TPU v7x, 32 devices: a whole 2x2x4 slice. The times are simulated.
32 devices in a mesh: bricks: 32 (over z, y, x, core).
Axes of the slice: x: 2, y: 2, z: 4, core: 2. Of those that a mesh axis runs over, the one named last changes fastest.
Arguments:
- fluid_state: float32 [18, 128, 8, 128], P(None, 'bricks'), as said below
- harmonics: bfloat16 [1681, 128, 8, 128], P(None, 'bricks'), may hold values from -6 to 6
- zone_slot: int32 [128, 8, 128], P('bricks'), may hold values from 0 to 255
- bin_list: int32 [32, 256], P('bricks'), may hold values from 0 to 1023, as said below
- shell_radius: float32 [1024], replicated, as said below
Outputs:
- new_state: float32 [18, 128, 8, 128], P(None, 'bricks')
- potential: float32 [128, 8, 128], P('bricks')
Inputs may be any that keep to these rules, and one draw needn't show every extreme that they name: `bin_list`: each row lists 256 distinct bins in rising order. `fluid_state`: density is positive, the x-momentum's magnitude is at most the density, and the densities of two zones beside each other along x differ by a factor of at most 32. `shell_radius`: positive and rising along the bins.
All inputs are finite; a program needn't handle non-finite values.
Results may differ from a plain program's by a relative error of at most 0.00065.
The roundings to bfloat16 on the way count: a program that leaves them out, or rounds other values in their place, can miss the bound.
Values may be sent and summed in bfloat16 or wider, within the bound.
A program may use at most 128 MiB of HBM per device.

v0:
```python
import math

import jax
import jax.numpy as jnp
from jax import lax
from jax.sharding import PartitionSpec as P

LMAX = 40
HARM = 1681
NB = 1024


time_step = 0.05


def padded_2(cells, sides, width):
    for axis, dim in sides:
        count = lax.axis_size(axis)
        ends = count - 1
        head = lax.slice_in_dim(cells, 0, width, axis=dim)
        tail = lax.slice_in_dim(cells, cells.shape[dim] - width, cells.shape[dim], axis=dim)
        cells = jnp.concatenate(
            [
                lax.ppermute(tail, axis, [(i, (i + 1) % count) for i in range(ends)]),
                cells,
                lax.ppermute(head, axis, [((i + 1) % count, i) for i in range(ends)]),
            ],
            axis=dim,
        )
    return cells


def prefix(value, axis, join, neutral, backward):
    count, mine = (lax.axis_size(axis), lax.axis_index(axis))
    pieces = jax.tree.map(lambda part: lax.all_gather(part, axis), value)
    if backward:
        pieces = jax.tree.map(lambda part: part[::-1], pieces)
        mine = count - 1 - mine
    running = jax.tree.map(
        lambda part, zero: jnp.full_like(part, 0) + jnp.asarray(zero, part.dtype), value, neutral
    )

    def hop(position, running):
        longer = join(running, jax.tree.map(lambda part: part[position], pieces))
        return jax.tree.map(lambda new, old: jnp.where(position < mine, new, old), longer, running)

    return lax.fori_loop(0, count - 1, hop, running)


def chain_link(first_pair, second_pair):
    return (first_pair[0] * second_pair[0], second_pair[0] * first_pair[1] + second_pair[1])


def degrees(harm_count):
    numbers = jnp.arange(harm_count, dtype=jnp.int32)
    marks = jnp.arange(1, LMAX + 1, dtype=jnp.int32) ** 2
    return jnp.sum((numbers[:, None] >= marks[None, :]).astype(jnp.int32), axis=1).astype(
        jnp.float32
    )


def log_steps(radius):
    bin_count = radius.shape[0]
    step_in = jnp.concatenate(
        [jnp.zeros((1,), radius.dtype), jnp.log(radius[:-1]) - jnp.log(radius[1:])]
    )
    step_out = jnp.concatenate([step_in[1:], jnp.zeros((1,), radius.dtype)])
    last_row = jnp.arange(bin_count, dtype=jnp.int32) == bin_count - 1
    return (step_in, step_out, last_row)


def own_chains(own_moments, shell_radius, degree, first_row):
    own_rows = own_moments.shape[0]
    step_in, step_out, last_row = log_steps(shell_radius)
    own_radius = lax.dynamic_slice_in_dim(shell_radius, first_row, own_rows)
    own_in = lax.dynamic_slice_in_dim(step_in, first_row, own_rows)
    own_out = lax.dynamic_slice_in_dim(step_out, first_row, own_rows)
    own_last = lax.dynamic_slice_in_dim(last_row, first_row, own_rows)
    scaled = own_moments / own_radius[:, None]
    grow_in = jnp.exp((degree[None, :] + 1.0) * own_in[:, None])
    grow_out = jnp.where(own_last[:, None], 0.0, jnp.exp(degree[None, :] * own_out[:, None]))
    inner_pre, inner_val = lax.associative_scan(chain_link, (grow_in, scaled))
    outer_pre, outer_val = lax.associative_scan(chain_link, (grow_out, scaled), reverse=True)
    return (scaled, inner_pre, inner_val, outer_pre, outer_val)


def join_chains(chains, carry_in, carry_out):
    scaled, inner_pre, inner_val, outer_pre, outer_val = chains
    inner = inner_val + inner_pre * carry_in[1][None]
    outer = outer_val + outer_pre * carry_out[1][None]
    return (inner + outer - scaled).astype(jnp.bfloat16)


def advance(fluid_state, padded, potential_padded, lower_bound, upper_bound):
    channels = fluid_state.shape[0]
    speed = padded[channels]
    fields = padded[:channels]
    face_flux = 0.25 * (speed[1:] + speed[:-1])[None] * (fields[:, 1:] + fields[:, :-1])
    advanced = fluid_state - time_step * (face_flux[:, 1:] - face_flux[:, :-1])
    gradient = 0.5 * (potential_padded[2:] - potential_padded[:-2])
    density = advanced[0]
    momentum = advanced[1] - time_step * fluid_state[0] * gradient
    energy = advanced[4] - time_step * fluid_state[1] * gradient
    fraction = jnp.clip(
        advanced[5:] / density[None],
        lower_bound[:, None, None, None],
        upper_bound[:, None, None, None],
    )
    return jnp.concatenate(
        [density[None], momentum[None], advanced[2:4], energy[None], density[None] * fraction],
        axis=0,
    )


def per_device(fluid_state, harmonics, zone_slot, bin_list, shell_radius):
    channels, width_x, width_y, width_z = fluid_state.shape
    harm_count = harmonics.shape[0]
    zone_count = width_x * width_y * width_z
    device_count = lax.axis_size("bricks")
    flat_harm = harmonics.reshape(harm_count, zone_count)
    slot_flat = zone_slot.reshape(zone_count)
    my_bins = bin_list[0]
    listed = my_bins.shape[0]
    velocity = fluid_state[1] / fluid_state[0]
    extended = jnp.concatenate([fluid_state, velocity[None]], axis=0)
    padded = padded_2(extended.astype(jnp.bfloat16), (("bricks", 1),), 1).astype(extended.dtype)
    fractions = fluid_state[5:] / fluid_state[0][None]
    local_low = jnp.min(fractions, axis=(1, 2, 3))
    local_high = jnp.max(fractions, axis=(1, 2, 3))
    extremes = lax.pmax(jnp.stack([-local_low, local_high]), "bricks")
    lower_bound = -extremes[0]
    upper_bound = extremes[1]
    mass = fluid_state[0].reshape(zone_count).astype(jnp.bfloat16)
    selector = jnp.arange(listed, dtype=jnp.int32)[:, None] == slot_flat[None, :]
    weights = jnp.where(selector, mass[None, :], jnp.zeros((), jnp.bfloat16))
    partial_value = lax.dot_general(
        weights, flat_harm, (((1,), (1,)), ((), ())), preferred_element_type=jnp.float32
    )
    degree = degrees(harm_count)
    unit = (jnp.ones((harm_count,), jnp.float32), jnp.zeros((harm_count,), jnp.float32))
    own_rows = NB // device_count
    first_row = lax.axis_index("bricks") * own_rows
    inside = (my_bins >= 0) & (my_bins < lax.axis_size("bricks") * own_rows)
    target = jnp.where(inside, my_bins, lax.axis_size("bricks") * own_rows)
    own_moments = lax.psum_scatter(
        jnp.zeros((lax.axis_size("bricks") * own_rows, harm_count), jnp.float32)
        .at[target]
        .add(partial_value, mode="drop"),
        "bricks",
        scatter_dimension=0,
        tiled=True,
    )
    chains = own_chains(own_moments, shell_radius, degree, first_row)
    carry_in = prefix((chains[1][-1], chains[2][-1]), "bricks", chain_link, unit, False)
    carry_out = prefix((chains[3][0], chains[4][0]), "bricks", chain_link, unit, True)
    own_shell = join_chains(chains, carry_in, carry_out)
    shard_rows = lax.all_gather(own_shell, "bricks", axis=0, tiled=True)
    row_total = shard_rows.shape[0]
    marks = (my_bins[:, None] == jnp.arange(row_total, dtype=jnp.int32)[None, :]).astype(
        jnp.bfloat16
    )
    picked = jnp.dot(marks, shard_rows, preferred_element_type=jnp.float32)
    shell_mine = picked.astype(jnp.bfloat16)
    product = jnp.dot(shell_mine, flat_harm, preferred_element_type=jnp.float32)
    factor = -1.0 / math.sqrt(float(HARM * zone_count * device_count))
    potential = (jnp.sum(jnp.where(selector, product, 0.0), axis=0) * factor).reshape(
        width_x, width_y, width_z
    )
    potential_padded = padded_2(potential, (("bricks", 0),), 1)
    new_state = advance(fluid_state, padded, potential_padded, lower_bound, upper_bound)
    return (new_state, potential)


def solution(mesh):
    placed = (
        P(None, "bricks", None, None),
        P(None, "bricks", None, None),
        P("bricks", None, None),
        P("bricks", None),
        P(),
    )
    return jax.shard_map(
        per_device,
        mesh=mesh,
        in_specs=placed,
        out_specs=(P(None, "bricks", None, None), P("bricks", None, None)),
        check_vma=False,
    )
```

profile of v0, /device:TPU:15, one launch (start us, length us, event | category | flops | bytes accessed | tf_op | source)
XLA Modules:
  0.0 471.9 jit_solution(6941772681292670749)
XLA Ops:
  7.2 7.8 %pad.232 = bf16[1688,32,128]{2,1,0:T(8,128)(2,1)S(1)} pad(bf16[1681,32,128]{2,1,0:T(8,128)(2,1)} %bitcast.86, bf16[]{:T(256)} %constant.73.clone.1), padding=0_7x0_0x0_0 | pad | bytes 27598850
  15.1 6.0 %copy.15 = bf16[211,8,32,128]{3,1,2,0:T(8,128)(2,1)S(1)} copy(bf16[211,8,32,128]{3,2,1,0:T(8,128)(2,1)S(1)} %bitcast.83) | data formatting | bytes 27656192
  21.2 4.0 fusion.3
  25.2 0.9 copy-done
  26.1 6.8 %scatter_custom_fusion = f32[1024,1681]{1,0:T(8,128)} fusion(s32[256]{0:T(256)S(1)} %bitcast.93, f32[256,1681]{1,0:T(8,128)S(1)} %fusion.3, f32[]{:T(128)} %constant.70.clone.1), kind=kCustom, calls=%fused_computation.10 | custom fusion | flops 430336 | bytes 6885380 | tf_op jit(solution)/shard_map/scatter-add | solution.py:148
  32.9 0.2 all-gather.6.cloned.1.call-start
  33.1 0.4 copy-done.5
  33.6 0.1 dynamic_slice.40
  33.6 0.1 log_subtract_fusion
  33.7 0.1 pad_maximum_fusion.20
  33.8 0.1 dynamic_slice.41
  33.9 0.1 convert_reduce_fusion
  34.0 0.1 multiply_exponential_fusion
  34.2 0.1 slice.421
  34.3 0.1 dynamic_slice.43
  34.4 0.1 dynamic_slice.42
  34.5 0.1 exponential_select_fusion
  34.8 0.2 slice.470
  35.0 0.2 slice.475
  35.3 0.4 slice.468
  35.6 115.1 %reduce-scatter.2.cloned.1.call-done = f32[32,1681]{1,0:T(8,128)} async-done(((f32[1024,1681]{1,0:T(8,128)}), f32[32,1681]{1,0:T(8,128)}) %reduce-scatter.2.cloned.1.call-update) | async-done | bytes 215184 | tf_op jit(solution)/shard_map/reduce_scatter | solution.py:145
  150.8 1.0 broadcast_divide_fusion
  152.7 0.1 slice.454
  152.7 0.2 slice.471
  153.0 0.2 slice.472
  154.7 0.4 slice.504
  156.3 58.2 %all-gather.1 = f32[32,1,1681]{2,1,0:T(1,128)S(1)} all-gather(f32[1,1,1681]{2,1,0:T(1,128)S(1)} %add_bitcast_fusion.2), channel_id=1, replica_groups=mesh['bricks'=32] {'bricks'}, dimensions={0}, use_global_device_ids=true | all-gather | bytes 221892 | tf_op jit(solution)/shard_map/all_gather | solution.py:35
  214.7 37.0 %all-gather = f32[32,1,1681]{2,1,0:T(1,128)S(1)} all-gather(f32[1,1,1681]{2,1,0:T(1,128)S(1)} %add_bitcast_fusion.3), channel_id=1, replica_groups=mesh['bricks'=32] {'bricks'}, dimensions={0}, use_global_device_ids=true | all-gather | bytes 221892 | tf_op jit(solution)/shard_map/all_gather | solution.py:35
  251.7 3.0 while.28
  251.8 0.1 dynamic-slice_reduce_fusion.6
  251.9 0.1 dynamic-slice_reduce_fusion.6
  252.4 0.1 dynamic-slice_reduce_fusion.6
  252.5 0.1 dynamic-slice_reduce_fusion.6
  253.0 0.1 dynamic-slice_reduce_fusion.6
  253.0 0.1 dynamic-slice_reduce_fusion.6
  253.6 0.1 dynamic-slice_reduce_fusion.6
  253.7 0.1 dynamic-slice_reduce_fusion.6
  254.2 0.1 dynamic-slice_reduce_fusion.6
  254.3 0.1 dynamic-slice_reduce_fusion.6
  254.7 38.9 %all-gather.3 = f32[32,1,1681]{2,1,0:T(1,128)S(1)} all-gather(f32[1,1,1681]{2,1,0:T(1,128)S(1)} %add_bitcast_fusion), channel_id=1, replica_groups=mesh['bricks'=32] {'bricks'}, dimensions={0}, use_global_device_ids=true | all-gather | bytes 221892 | tf_op jit(solution)/shard_map/all_gather | solution.py:35
  293.6 0.3 rev.17
  293.8 37.3 %all-gather.2 = f32[32,1,1681]{2,1,0:T(1,128)S(1)} all-gather(f32[1,1,1681]{2,1,0:T(1,128)S(1)} %add_bitcast_fusion.1), channel_id=1, replica_groups=mesh['bricks'=32] {'bricks'}, dimensions={0}, use_global_device_ids=true | all-gather | bytes 221892 | tf_op jit(solution)/shard_map/all_gather | solution.py:35
  331.1 0.3 rev.16
  331.4 3.0 while.29
  331.7 0.1 dynamic-slice_reduce_fusion.7
  331.9 0.1 dynamic-slice_reduce_fusion.7
  332.1 0.1 dynamic-slice_reduce_fusion.7
  334.4 0.3 rev.15
  334.6 0.3 rev.14
  334.9 0.8 subtract_convert_fusion
  335.7 3.4 collective-permute-start
  339.1 1.9 collective-permute-start.1
  341.1 5.2 %collective-permute-done.1 = bf16[19,1,8,128]{3,2,1,0:T(8,128)(2,1)S(1)} collective-permute-done((bf16[19,1,8,128]{3,2,1,0:T(8,128)(2,1)S(1)}, bf16[19,1,8,128]{3,2,1,0:T(8,128)(2,1)S(1)}, u32[]{:S(2)}, u32[]{:S(2)}) %collective-permute-start.1) | collective-permute-done | bytes 38944 | tf_op jit(solution)/shard_map/ppermute | solution.py:26
  346.2 0.1 maximum_convert_fusion
  346.3 0.1 fusion.13
  346.4 55.7 %all-gather.6.cloned.1.call-done = bf16[1024,1681]{1,0:T(8,128)(2,1)} async-done(((bf16[32,1681]{1,0:T(8,128)(2,1)}), bf16[1024,1681]{1,0:T(8,128)(2,1)}) %all-gather.6.cloned.1.call-update) | async-done | bytes 3442704 | tf_op jit(solution)/shard_map/all_gather | solution.py:157
  402.1 13.8 %fusion.6 = f32[4096]{0:T(1024)S(1)} fusion(bf16[1681,4096]{1,0:T(8,128)(2,1)} %bitcast.85, s32[4096]{0:T(1024)S(1)} %bitcast.95, bf16[1024,1681]{1,0:T(8,128)(2,1)} %all-gather.6.cloned.1.call-done, s32[256]{0:T(256)S(1)} %bitcast.92), kind=kOutput, calls=%fused_computation.15 | convolution fusion | flops 4410474496 | bytes 17247232 | tf_op jit(solution)/shard_map/dot_general | solution.py:164
  415.9 2.2 collective-permute-start.2
  418.1 5.2 %collective-permute-start.3 = (f32[1,8,128]{2,1,0:T(8,128)S(1)}, f32[1,8,128]{2,1,0:T(8,128)S(1)}, u32[]{:S(2)}, u32[]{:S(2)}) collective-permute-start(f32[1,8,128]{2,1,0:T(8,128)S(1)} %get-tuple-element.295), channel_id=1, source_target_pairs={{0,1},{1,2},{2,3},{3,4},{4,5},{5,6},{6,7},{7,8},{8,9},{9,10},{10,1... | collective-permute-start | bytes 12296 | tf_op jit(solution)/shard_map/ppermute | solution.py:24
  423.3 0.7 collective-permute-done.3
  424.1 0.2 fusion.21
  424.3 40.0 %pmax.7 = f32[2,13]{1,0:T(2,128)S(1)} all-reduce(f32[2,13]{1,0:T(2,128)S(1)} %pad_maximum_fusion.22), channel_id=1, replica_groups=mesh['bricks'=32] {'bricks'}, use_global_device_ids=true, to_apply=%region_10.11 | all-reduce | flops 26 | bytes 208 | tf_op jit(solution)/shard_map/pmax | solution.py:130
  464.3 0.1 fusion.17
  464.4 0.7 copy-done.7
  (293 shorter events, 6.6 us)
Async XLA Ops:
  7.2 143.6 %reduce-scatter.2.cloned.1.call-start = ((), (), s32[]{:S(2)}) async-start(), calls=%async_computation.1 | async-start | bytes 7569408 | tf_op jit(solution)/shard_map/reduce_scatter | solution.py:145
  15.1 6.1 %copy-start.1 = (f32[18,4,8,128]{3,2,1,0:T(8,128)S(1)}, f32[18,4,8,128]{3,2,1,0:T(8,128)}, u32[]{:S(2)}) copy-start(f32[18,4,8,128]{3,2,1,0:T(8,128)} %param.9) | copy-start | bytes 884740
  15.1 6.1 %copy-start.6 = (s32[1,256]{1,0:T(1,128)S(1)}, s32[1,256]{1,0:T(1,128)}, u32[]{:S(2)}) copy-start(s32[1,256]{1,0:T(1,128)} %param.12) | copy-start | bytes 3076
  15.1 6.1 %copy-start.8 = (s32[4,8,128]{2,1,0:T(8,128)S(1)}, s32[4,8,128]{2,1,0:T(8,128)}, u32[]{:S(2)}) copy-start(s32[4,8,128]{2,1,0:T(8,128)} %param.11) | copy-start | bytes 49156
  21.2 5.0 %copy-start = (bf16[211,8,32,128]{3,1,2,0:T(8,128)(2,1)}, bf16[211,8,32,128]{3,1,2,0:T(8,128)(2,1)S(1)}, u32[]{:S(2)}) copy-start(bf16[211,8,32,128]{3,1,2,0:T(8,128)(2,1)S(1)} %copy.15) | copy-start | bytes 41484292
  32.9 0.7 copy-start.5
  32.9 369.2 %all-gather.6.cloned.1.call-start = ((), (), s32[]{:S(2)}) async-start(), calls=%async_computation.2 | async-start | bytes 3784704 | tf_op jit(solution)/shard_map/all_gather | solution.py:157
  34.1 119.4 %copy-start.2 = (f32[32,1681]{1,0:T(8,128)}, f32[32,1681]{1,0:T(8,128)S(1)}, u32[]{:S(2)}) copy-start(f32[32,1681]{1,0:T(8,128)S(1)} %multiply_exponential_fusion) | copy-start | bytes 645508
  155.3 59.3 %slice-start = ((f32[32,1681]{1,0:T(8,128)}), f32[1,1681]{1,0:T(1,128)S(1)}, s32[]{:S(2)}) async-start(f32[32,1681]{1,0:T(8,128)} %copy-done.2), calls=%async_computation.3 | async-start | bytes 14336 | tf_op jit(solution)/shard_map/slice | solution.py:82
  156.2 178.7 %copy-start.3 = (f32[32,1681]{1,0:T(8,128)S(1)}, f32[32,1681]{1,0:T(8,128)}, u32[]{:S(2)}) copy-start(f32[32,1681]{1,0:T(8,128)} %reduce-scatter.2.cloned.1.call-done) | copy-start | bytes 645508
  335.7 5.3 %collective-permute-start = (bf16[19,1,8,128]{3,2,1,0:T(8,128)(2,1)S(1)}, bf16[19,1,8,128]{3,2,1,0:T(8,128)(2,1)S(1)}, u32[]{:S(2)}, u32[]{:S(2)}) collective-permute-start(bf16[19,1,8,128]{3,2,1,0:T(8,128)(2,1)S(1)} %get-tuple-element.260), channel_id=1, source_target_pairs={{0,1},{1,2},{2,3},{3,4},{4,5},{5,6},{6,7},{7,8},{8,9},{9,10},{10,1... | collective-permute-start | bytes 116744 | tf_op jit(solution)/shard_map/ppermute | solution.py:24
  339.1 7.1 %collective-permute-start.1 = (bf16[19,1,8,128]{3,2,1,0:T(8,128)(2,1)S(1)}, bf16[19,1,8,128]{3,2,1,0:T(8,128)(2,1)S(1)}, u32[]{:S(2)}, u32[]{:S(2)}) collective-permute-start(bf16[19,1,8,128]{3,2,1,0:T(8,128)(2,1)S(1)} %get-tuple-element.261), channel_id=1, source_target_pairs={{1,0},{2,1},{3,2},{4,3},{5,4},{6,5},{7,6},{8,7},{9,8},{10,9},{11,1... | collective-permute-start | bytes 116744 | tf_op jit(solution)/shard_map/ppermute | solution.py:26
  415.9 48.5 %copy-start.4 = (f32[4,8,128]{2,1,0:T(8,128)}, f32[4,8,128]{2,1,0:T(8,128)S(1)}, u32[]{:S(2)}) copy-start(f32[4,8,128]{2,1,0:T(8,128)S(1)} %get-tuple-element.297) | copy-start | bytes 49156
  415.9 7.4 %collective-permute-start.2 = (f32[1,8,128]{2,1,0:T(8,128)S(1)}, f32[1,8,128]{2,1,0:T(8,128)S(1)}, u32[]{:S(2)}, u32[]{:S(2)}) collective-permute-start(f32[1,8,128]{2,1,0:T(8,128)S(1)} %get-tuple-element.294), channel_id=1, source_target_pairs={{1,0},{2,1},{3,2},{4,3},{5,4},{6,5},{7,6},{8,7},{9,8},{10,9},{11,1... | collective-permute-start | bytes 12296 | tf_op jit(solution)/shard_map/ppermute | solution.py:26
  418.1 5.9 %collective-permute-start.3 = (f32[1,8,128]{2,1,0:T(8,128)S(1)}, f32[1,8,128]{2,1,0:T(8,128)S(1)}, u32[]{:S(2)}, u32[]{:S(2)}) collective-permute-start(f32[1,8,128]{2,1,0:T(8,128)S(1)} %get-tuple-element.295), channel_id=1, source_target_pairs={{0,1},{1,2},{2,3},{3,4},{4,5},{5,6},{6,7},{7,8},{8,9},{9,10},{10,1... | collective-permute-start | bytes 12296 | tf_op jit(solution)/shard_map/ppermute | solution.py:24
  464.4 0.7 copy-start.7
Sparse Core Ops, SparseCore 0:
  33.0 117.6 reduce-scatter.1
  335.8 66.2 all-gather.5
where the time goes:
time: 476 us; the launch traced here: 472 us
  blocking collectives  211 us (44%)
  waiting for transfers between devices  177 us (37%)
  local copies, waits for them, and re-layouts  24.4 us (5%)
  matrix products  17.8 us (4%)
  between operations  15.3 us (3%)
  starting transfers between devices  12.9 us (3%)
  other arithmetic  11.2 us (2%)
    all_gather x4, blocking collectives, prefix(): pieces = jax.tree.map(lambda part: lax.all_gather(part, axis), value)  171 us
    reduce_scatter x1, waiting for transfers between devices, per_device(): lax.psum_scatter(jnp.zeros((lax.axis_size('bricks') * own_rows, harm_coun...  115 us
    all_gather x1, waiting for transfers between devices, per_device(): shard_rows = lax.all_gather(own_shell, 'bricks', axis=0, tiled=True)  55.7 us
    pmax x1, blocking collectives, per_device(): extremes = lax.pmax(jnp.stack([-local_low, local_high]), 'bricks')  40 us
    unnamed x25, local copies, waits for them, and re-layouts  16.1 us
    dot_general x1, matrix products, per_device(): product = jnp.dot(shell_mine, flat_harm, preferred_element_type=jnp.float32)  13.8 us
  transfers between devices with their start and end apart: 6, of which 4 were waited for; matrix products, arithmetic and copies ran while one was open for 0% of the time, Pallas kernels for 0%

commit v1 on v0

v1 whole, which is shorter than its diff:
```python
import functools
import math

import jax
import jax.numpy as jnp
from jax import lax
from jax.experimental import pallas as pl
from jax.experimental.pallas import tpu as pltpu
from jax.sharding import PartitionSpec as P

LMAX = 40
HARM = 1681
NB = 1024


MESH = pl.DeviceIdType.MESH

time_step = 0.05


def padded_2(cells, sides, width):
    for axis, dim in sides:
        count = lax.axis_size(axis)
        ends = count - 1
        head = lax.slice_in_dim(cells, 0, width, axis=dim)
        tail = lax.slice_in_dim(cells, cells.shape[dim] - width, cells.shape[dim], axis=dim)
        cells = jnp.concatenate(
            [
                lax.ppermute(tail, axis, [(i, (i + 1) % count) for i in range(ends)]),
                cells,
                lax.ppermute(head, axis, [((i + 1) % count, i) for i in range(ends)]),
            ],
            axis=dim,
        )
    return cells


def degrees(harm_count):
    numbers = jnp.arange(harm_count, dtype=jnp.int32)
    marks = jnp.arange(1, LMAX + 1, dtype=jnp.int32) ** 2
    return jnp.sum((numbers[:, None] >= marks[None, :]).astype(jnp.int32), axis=1).astype(
        jnp.float32
    )


def log_steps(radius):
    bin_count = radius.shape[0]
    step_in = jnp.concatenate(
        [jnp.zeros((1,), radius.dtype), jnp.log(radius[:-1]) - jnp.log(radius[1:])]
    )
    step_out = jnp.concatenate([step_in[1:], jnp.zeros((1,), radius.dtype)])
    last_row = jnp.arange(bin_count, dtype=jnp.int32) == bin_count - 1
    return (step_in, step_out, last_row)


def round_up(value, step):
    return -(-value // step) * step


def one_hot(bin_row, row_total, listed):
    rows = lax.broadcasted_iota(jnp.int32, (row_total, listed), 0)
    return jnp.where(rows == bin_row, 1.0, 0.0).astype(jnp.bfloat16)


def exchange_kernel(
    n, group, part_ref, small_ref, grow_in_ref, grow_out_ref, radius_ref,
    shell_ref, extreme_ref,
    got, smalls, total, shell_t, sent_back, came_back,
    small_send, small_recv, part_send, part_recv, back_send, back_recv,
):
    me = lax.axis_index("bricks")
    block = part_ref.shape[1]
    listed = part_ref.shape[2]
    rows = radius_ref.shape[0]
    back_rows = sent_back.shape[1]

    def peer(offset):
        return lax.rem(me + offset, n)

    def source(offset):
        return lax.rem(me - offset + n, n)

    barrier = pltpu.get_barrier_semaphore()

    def greet(offset, carry):
        pl.semaphore_signal(barrier, inc=1, device_id=(peer(offset),), device_id_type=MESH)
        return carry

    lax.fori_loop(1, n, greet, 0)
    smalls[me] = small_ref[...]
    got[me] = part_ref[me]
    total[...] = jnp.zeros_like(total)
    pl.semaphore_wait(barrier, n - 1)

    def small_copy(target, slot):
        return pltpu.make_async_remote_copy(
            src_ref=small_ref, dst_ref=smalls.at[slot], send_sem=small_send.at[target],
            recv_sem=small_recv.at[slot], device_id=(target,), device_id_type=MESH)

    def part_copy(target, slot):
        return pltpu.make_async_remote_copy(
            src_ref=part_ref.at[target], dst_ref=got.at[slot], send_sem=part_send.at[target],
            recv_sem=part_recv.at[slot], device_id=(target,), device_id_type=MESH)

    def back_copy(target, slot):
        return pltpu.make_async_remote_copy(
            src_ref=sent_back.at[target], dst_ref=came_back.at[slot], send_sem=back_send.at[target],
            recv_sem=back_recv.at[slot], device_id=(target,), device_id_type=MESH)

    def send_parts(offset, carry):
        small_copy(peer(offset), me).start()
        part_copy(peer(offset), me).start()
        return carry

    lax.fori_loop(1, n, send_parts, 0)

    def arrive(offset):
        small_copy(peer(offset), source(offset)).wait_recv()
        part_copy(peer(offset), source(offset)).wait_recv()

    def add_group(number, carry):
        for member in range(group):
            offset = number * group + member

            @pl.when(offset > 0)
            def _():
                arrive(offset)

        marks, halves = [], []
        for member in range(group):
            origin = source(number * group + member)
            marks.append(one_hot(smalls[origin, 0:1, :].astype(jnp.int32), rows, listed))
            values = got[origin]
            high = values.astype(jnp.bfloat16).astype(jnp.float32)
            gap = jnp.zeros((64 - block, listed), jnp.float32)
            halves.append(
                jnp.concatenate([high, gap, values - high, gap], axis=0).astype(jnp.bfloat16)
            )
        total[...] += lax.dot_general(
            jnp.concatenate(marks, axis=1), jnp.concatenate(halves, axis=1),
            (((1,), (1,)), ((), ())), preferred_element_type=jnp.float32)
        return carry

    lax.fori_loop(0, n // group, add_group, 0)
    extreme_ref[...] = jnp.max(smalls[...], axis=0)
    both = total[...]
    scaled = (both + pltpu.roll(both, 64, 1)) / radius_ref[...]
    field = -scaled
    for grow_ref, backward in ((grow_in_ref, False), (grow_out_ref, True)):
        factor, value = grow_ref[...], scaled
        step = 1
        while step < rows:
            turn = rows - step if backward else step
            value = value + factor * pltpu.roll(value, turn, 0)
            factor = factor * pltpu.roll(factor, turn, 0)
            step *= 2
        field = field + value
    shell_t[...] = field.T.astype(jnp.bfloat16)

    def select(target):
        marks = one_hot(smalls[target, 0:1, :].astype(jnp.int32), rows, listed)
        return jnp.dot(
            shell_t[0:back_rows, :], marks, preferred_element_type=jnp.float32
        ).astype(jnp.bfloat16)

    def send_back(offset, carry):
        target = peer(offset)
        sent_back[target] = select(target)
        back_copy(target, me).start()
        return carry

    lax.fori_loop(1, n, send_back, 0)
    shell_ref[me] = select(me)

    def finish(offset, carry):
        small_copy(peer(offset), me).wait_send()
        part_copy(peer(offset), me).wait_send()
        back_copy(peer(offset), me).wait_send()
        origin = source(offset)
        back_copy(peer(offset), origin).wait_recv()
        shell_ref[origin] = came_back[origin]
        return carry

    lax.fori_loop(1, n, finish, 0)


def exchange(parts, small, grow_in, grow_out, radius):
    n, block, listed = parts.shape
    rows = radius.shape[0]
    back_rows = round_up(block, 16)
    whole = pl.BlockSpec(memory_space=pltpu.VMEM)
    return pl.pallas_call(
        functools.partial(exchange_kernel, n, 4),
        out_shape=(
            jax.ShapeDtypeStruct((n, back_rows, listed), jnp.bfloat16),
            jax.ShapeDtypeStruct(small.shape, jnp.float32),
        ),
        in_specs=[whole] * 5,
        out_specs=(whole, whole),
        scratch_shapes=[
            pltpu.VMEM((n, block, listed), jnp.float32),
            pltpu.VMEM((n,) + small.shape, jnp.float32),
            pltpu.VMEM((rows, 128), jnp.float32),
            pltpu.VMEM((128, rows), jnp.bfloat16),
            pltpu.VMEM((n, back_rows, listed), jnp.bfloat16),
            pltpu.VMEM((n, back_rows, listed), jnp.bfloat16),
        ] + [pltpu.SemaphoreType.DMA((n,))] * 6,
        compiler_params=pltpu.CompilerParams(
            collective_id=0, has_side_effects=True, vmem_limit_bytes=48 * 1024 * 1024
        ),
    )(parts, small, grow_in, grow_out, radius)


def advance(fluid_state, padded, potential_padded, lower_bound, upper_bound):
    channels = fluid_state.shape[0]
    speed = padded[channels]
    fields = padded[:channels]
    face_flux = 0.25 * (speed[1:] + speed[:-1])[None] * (fields[:, 1:] + fields[:, :-1])
    advanced = fluid_state - time_step * (face_flux[:, 1:] - face_flux[:, :-1])
    gradient = 0.5 * (potential_padded[2:] - potential_padded[:-2])
    density = advanced[0]
    momentum = advanced[1] - time_step * fluid_state[0] * gradient
    energy = advanced[4] - time_step * fluid_state[1] * gradient
    fraction = jnp.clip(
        advanced[5:] / density[None],
        lower_bound[:, None, None, None],
        upper_bound[:, None, None, None],
    )
    return jnp.concatenate(
        [density[None], momentum[None], advanced[2:4], energy[None], density[None] * fraction],
        axis=0,
    )


def per_device(fluid_state, harmonics, zone_slot, bin_list, shell_radius):
    channels, width_x, width_y, width_z = fluid_state.shape
    harm_count = harmonics.shape[0]
    zone_count = width_x * width_y * width_z
    device_count = lax.axis_size("bricks")
    flat_harm = harmonics.reshape(harm_count, zone_count)
    slot_flat = zone_slot.reshape(zone_count)
    my_bins = bin_list[0]
    listed = my_bins.shape[0]
    velocity = fluid_state[1] / fluid_state[0]
    extended = jnp.concatenate([fluid_state, velocity[None]], axis=0)
    padded = padded_2(extended.astype(jnp.bfloat16), (("bricks", 1),), 1).astype(extended.dtype)
    fractions = fluid_state[5:] / fluid_state[0][None]
    local_low = jnp.min(fractions, axis=(1, 2, 3))
    local_high = jnp.max(fractions, axis=(1, 2, 3))
    mass = fluid_state[0].reshape(zone_count).astype(jnp.bfloat16)
    selector = jnp.arange(listed, dtype=jnp.int32)[:, None] == slot_flat[None, :]
    weights = jnp.where(selector, mass[None, :], jnp.zeros((), jnp.bfloat16))
    partial_value = lax.dot_general(
        flat_harm, weights, (((1,), (1,)), ((), ())), preferred_element_type=jnp.float32
    )
    block = round_up(-(-harm_count // device_count), 8)
    padded_count = block * device_count
    parts = jnp.pad(partial_value, ((0, padded_count - harm_count), (0, 0))).reshape(
        device_count, block, listed
    )
    species = local_low.shape[0]
    extreme_row = jnp.pad(jnp.concatenate([-local_low, local_high]), (0, listed - 2 * species))
    small = jnp.pad(
        jnp.stack([my_bins.astype(jnp.float32), extreme_row]), ((0, 6), (0, 0))
    )
    own_degree = lax.dynamic_slice_in_dim(
        jnp.pad(degrees(harm_count), (0, padded_count + 128 - harm_count)),
        lax.axis_index("bricks") * block, 128)
    step_in, step_out, last_row = log_steps(shell_radius)
    first = jnp.arange(NB, dtype=jnp.int32) == 0
    grow_in = jnp.where(first[:, None], 0.0, jnp.exp((own_degree[None, :] + 1.0) * step_in[:, None]))
    grow_out = jnp.where(last_row[:, None], 0.0, jnp.exp(own_degree[None, :] * step_out[:, None]))
    radius = jnp.broadcast_to(shell_radius[:, None], (NB, 128))
    shells, extremes = exchange(parts, small, grow_in, grow_out, radius)
    lower_bound = -extremes[1, :species]
    upper_bound = extremes[1, species : 2 * species]
    shell_mine = shells[:, :block].reshape(padded_count, listed)[:harm_count].T
    product = jnp.dot(shell_mine, flat_harm, preferred_element_type=jnp.float32)
    factor = -1.0 / math.sqrt(float(HARM * zone_count * device_count))
    potential = (jnp.sum(jnp.where(selector, product, 0.0), axis=0) * factor).reshape(
        width_x, width_y, width_z
    )
    potential_padded = padded_2(potential, (("bricks", 0),), 1)
    new_state = advance(fluid_state, padded, potential_padded, lower_bound, upper_bound)
    return (new_state, potential)


def solution(mesh):
    placed = (
        P(None, "bricks", None, None),
        P(None, "bricks", None, None),
        P("bricks", None, None),
        P("bricks", None),
        P(),
    )
    return jax.shard_map(
        per_device,
        mesh=mesh,
        in_specs=placed,
        out_specs=(P(None, "bricks", None, None), P("bricks", None, None)),
        check_vma=False,
    )
```

time: 476 us -> 146 us (0.31)
  blocking collectives: 211 us -> 0 us
  waiting for transfers between devices: 177 us -> 4.51 us
  Pallas kernels: 0 us -> 84.9 us
  between operations: 15.3 us -> 0.93 us
  other arithmetic: 11.2 us -> 3.35 us
  local copies, waits for them, and re-layouts: 24.4 us -> 19.4 us
    all_gather x4 -> x0, blocking collectives: 171 us -> none  [prefix(): pieces = jax.tree.map(lambda part: lax.all_gather(part, axis), value)]
    reduce_scatter x1 -> x0, waiting for transfers between devices: 115 us -> none  [per_device(): lax.psum_scatter(jnp.zeros((lax.axis_size('bricks') * own_rows, harm_coun...]
    pallas_call x0 -> x1, Pallas kernels: none -> 84.9 us  [exchange(): pl.pallas_call(functools.partial(exchange_kernel, n, 4), out_shape=(jax.S...]
    all_gather x1 -> x0, waiting for transfers between devices: 55.7 us -> none  [per_device(): shard_rows = lax.all_gather(own_shell, 'bricks', axis=0, tiled=True)]
    pmax x1 -> x0, blocking collectives: 40 us -> none  [per_device(): extremes = lax.pmax(jnp.stack([-local_low, local_high]), 'bricks')]
    scatter-add x1 -> x0, other arithmetic: 6.75 us -> none  [per_device(): own_moments = lax.psum_scatter(jnp.zeros((lax.axis_size('bricks') * own_r...]
    unnamed x25 -> x15, local copies, waits for them, and re-layouts: 16.1 us -> 18.3 us
  transfers between devices with their start and end apart: 6 -> 4, of which waited for: 4 -> 1; matrix products, arithmetic and copies ran while one was open for 0% -> 26% of each run, Pallas kernels for 0% -> 59%
where the time goes in v1:
time: 146 us; the launch traced here: 144 us
  Pallas kernels  84.9 us (58%)
  local copies, waits for them, and re-layouts  19.4 us (13%)
  matrix products  16.8 us (12%)
  starting transfers between devices  14.5 us (10%)
  waiting for transfers between devices  4.51 us (3%)
  other arithmetic  3.35 us (2%)
    pallas_call x1, Pallas kernels, exchange(): pl.pallas_call(functools.partial(exchange_kernel, n, 4), out_shape=(jax.S...  84.9 us
    unnamed x15, local copies, waits for them, and re-layouts  18.3 us
    ppermute x2, starting transfers between devices, padded_2(): lax.ppermute(tail, axis, [(i, (i + 1) % count) for i in range(ends)])  10 us
    dot_general x1, matrix products, per_device(): product = jnp.dot(shell_mine, flat_harm, preferred_element_type=jnp.float32)  9.66 us
    dot_general x1, matrix products, per_device(): lax.dot_general(flat_harm, weights, (((1,), (1,)), ((), ())), preferred_e...  7.1 us
    ppermute x2, waiting for transfers between devices, padded_2(): lax.ppermute(head, axis, [((i + 1) % count, i) for i in range(ends)])  4.51 us
    ppermute x2, starting transfers between devices, padded_2(): lax.ppermute(head, axis, [((i + 1) % count, i) for i in range(ends)])  4.5 us
  transfers between devices with their start and end apart: 4, of which 1 were waited for; matrix products, arithmetic and copies ran while one was open for 26% of the time, Pallas kernels for 59%

profile of v1, /device:TPU:15, one launch (start us, length us, event | category | flops | bytes accessed | tf_op | source)
XLA Modules:
  0.0 144.3 jit_solution(5659152541714522066)
XLA Ops:
  0.6 0.7 slice_bitcast_fusion.3
  1.4 1.0 convert.6
  2.4 2.6 %collective-permute-start.1 = (bf16[19,1,8,128]{3,2,1,0:T(8,128)(2,1)S(1)}, bf16[19,1,8,128]{3,2,1,0:T(8,128)(2,1)S(1)}, u32[]{:S(2)}, u32[]{:S(2)}) collective-permute-start(bf16[19,1,8,128]{3,2,1,0:T(8,128)(2,1)S(1)} %get-tuple-element.15), channel_id=1, source_target_pairs={{1,0},{2,1},{3,2},{4,3},{5,4},{6,5},{7,6},{8,7},{9,8},{10,9},{11,1... | collective-permute-start | bytes 116744 | tf_op jit(solution)/shard_map/ppermute | solution.py:31
  5.0 4.8 %collective-permute-start = (bf16[19,1,8,128]{3,2,1,0:T(8,128)(2,1)S(1)}, bf16[19,1,8,128]{3,2,1,0:T(8,128)(2,1)S(1)}, u32[]{:S(2)}, u32[]{:S(2)}) collective-permute-start(bf16[19,1,8,128]{3,2,1,0:T(8,128)(2,1)S(1)} %get-tuple-element.14), channel_id=1, source_target_pairs={{0,1},{1,2},{2,3},{3,4},{4,5},{5,6},{6,7},{7,8},{8,9},{9,10},{10,1... | collective-permute-start | bytes 116744 | tf_op jit(solution)/shard_map/ppermute | solution.py:29
  9.8 0.7 fusion.26
  10.5 7.8 %pad.58 = bf16[1688,32,128]{2,1,0:T(8,128)(2,1)S(1)} pad(bf16[1681,32,128]{2,1,0:T(8,128)(2,1)} %bitcast.64, bf16[]{:T(256)} %constant.18.clone.1), padding=0_7x0_0x0_0 | pad | bytes 27598850
  18.4 0.0 copy-start
  18.4 0.0 copy-start.3
  18.4 0.0 copy-start.2
  18.4 0.0 copy-start.5
  18.4 9.7 %copy.7 = bf16[211,8,32,128]{3,1,2,0:T(8,128)(2,1)} copy(bf16[211,8,32,128]{3,2,1,0:T(8,128)(2,1)S(1)} %bitcast.61) | data formatting | bytes 27656192
  28.1 0.0 copy-done
  28.1 0.2 fusion.15
  28.3 0.0 copy-done.3
  28.3 0.0 copy-done.2
  28.3 0.1 log_subtract_fusion
  28.4 0.1 convert_reduce_fusion
  28.5 0.0 copy-done.5
  28.5 7.1 %convolution_bitcast_fusion = f32[1681,256]{1,0:T(8,128)S(1)} fusion(bf16[1681,4096]{1,0:T(8,128)(2,1)} %bitcast.62, s32[4096]{0:T(1024)S(1)} %bitcast.67, bf16[4096]{0:T(1024)(128)(2,1)S(1)} %fusion.26), kind=kOutput, calls=%fused_computation.3 | convolution fusion | flops 3527409664 | bytes 15516672 | tf_op jit(solution)/shard_map/dot_general | solution.py:253
  35.6 0.1 pad.16
  35.8 0.1 select_maximum_fusion.1
  35.8 0.1 pad_maximum_fusion.5
  35.9 0.1 broadcast_add_fusion
  36.0 0.6 exponential_select_fusion
  36.6 0.2 broadcast_in_dim.64.radius_ref
  36.8 84.9 %shard_map.68 = (bf16[32,64,256]{2,1,0:T(8,128)(2,1)S(1)}, f32[8,256]{1,0:T(8,128)S(1)}) custom-call(f32[32,56,256]{2,1,0:T(8,128)S(1)} %bitcast.60, f32[8,256]{1,0:T(8,128)S(1)} %select_maximum_fusion.small_ref, f32[1024,128]{1,0:T(8,128)S(1)} %get-tuple-element.25.grow_in_ref, f32[1024,128]{1,0:T(8,128)S(1)} %get-tuple-element.24.grow_out_ref, ...), custom_call_target="tpu_custom_call" | custom-call | tf_op jit(solution)/shard_map/pallas_call | solution.py:192
  121.7 0.1 slice.117
  121.8 9.7 %fusion.3 = f32[4096]{0:T(1024)S(1)} fusion(bf16[1681,4096]{1,0:T(8,128)(2,1)} %bitcast.63, s32[4096]{0:T(1024)S(1)} %bitcast.68, bf16[1792,256]{1,0:T(8,128)(2,1)S(1)} %bitcast.65), kind=kOutput, calls=%fused_computation.5 | convolution fusion | flops 3528454144 | bytes 14667776 | tf_op jit(solution)/shard_map/dot_general | solution.py:278
  131.4 0.0 copy-start.1
  131.5 5.2 %collective-permute-start.3 = (f32[1,8,128]{2,1,0:T(8,128)S(1)}, f32[1,8,128]{2,1,0:T(8,128)S(1)}, u32[]{:S(2)}, u32[]{:S(2)}) collective-permute-start(f32[1,8,128]{2,1,0:T(8,128)S(1)} %get-tuple-element.17), channel_id=1, source_target_pairs={{0,1},{1,2},{2,3},{3,4},{4,5},{5,6},{6,7},{7,8},{8,9},{9,10},{10,1... | collective-permute-start | bytes 12296 | tf_op jit(solution)/shard_map/ppermute | solution.py:29
  136.7 1.9 %collective-permute-start.2 = (f32[1,8,128]{2,1,0:T(8,128)S(1)}, f32[1,8,128]{2,1,0:T(8,128)S(1)}, u32[]{:S(2)}, u32[]{:S(2)}) collective-permute-start(f32[1,8,128]{2,1,0:T(8,128)S(1)} %get-tuple-element.16), channel_id=1, source_target_pairs={{1,0},{2,1},{3,2},{4,3},{5,4},{6,5},{7,6},{8,7},{9,8},{10,9},{11,1... | collective-permute-start | bytes 12296 | tf_op jit(solution)/shard_map/ppermute | solution.py:31
  138.7 0.1 slice_bitcast_fusion.6
  138.7 0.0 collective-permute-done.1
  138.7 0.0 collective-permute-done
  138.7 0.1 maximum_convert_fusion
  138.9 0.1 fusion.9
  138.9 0.0 collective-permute-done.3
  138.9 4.5 %collective-permute-done.2 = f32[1,8,128]{2,1,0:T(8,128)S(1)} collective-permute-done((f32[1,8,128]{2,1,0:T(8,128)S(1)}, f32[1,8,128]{2,1,0:T(8,128)S(1)}, u32[]{:S(2)}, u32[]{:S(2)}) %collective-permute-start.2) | collective-permute-done | bytes 4128 | tf_op jit(solution)/shard_map/ppermute | solution.py:31
  143.5 0.1 fusion.13
  143.6 0.0 copy-done.1
  143.6 0.0 copy-start.4
  143.6 0.7 copy-done.4
  (16 shorter events, 0.1 us)
Async XLA Ops:
  2.4 136.3 %collective-permute-start.1 = (bf16[19,1,8,128]{3,2,1,0:T(8,128)(2,1)S(1)}, bf16[19,1,8,128]{3,2,1,0:T(8,128)(2,1)S(1)}, u32[]{:S(2)}, u32[]{:S(2)}) collective-permute-start(bf16[19,1,8,128]{3,2,1,0:T(8,128)(2,1)S(1)} %get-tuple-element.15), channel_id=1, source_target_pairs={{1,0},{2,1},{3,2},{4,3},{5,4},{6,5},{7,6},{8,7},{9,8},{10,9},{11,1... | collective-permute-start | bytes 116744 | tf_op jit(solution)/shard_map/ppermute | solution.py:31
  5.0 133.8 %collective-permute-start = (bf16[19,1,8,128]{3,2,1,0:T(8,128)(2,1)S(1)}, bf16[19,1,8,128]{3,2,1,0:T(8,128)(2,1)S(1)}, u32[]{:S(2)}, u32[]{:S(2)}) collective-permute-start(bf16[19,1,8,128]{3,2,1,0:T(8,128)(2,1)S(1)} %get-tuple-element.14), channel_id=1, source_target_pairs={{0,1},{1,2},{2,3},{3,4},{4,5},{5,6},{6,7},{7,8},{8,9},{9,10},{10,1... | collective-permute-start | bytes 116744 | tf_op jit(solution)/shard_map/ppermute | solution.py:29
  18.4 9.7 %copy-start = (f32[18,4,8,128]{3,2,1,0:T(8,128)S(1)}, f32[18,4,8,128]{3,2,1,0:T(8,128)}, u32[]{:S(2)}) copy-start(f32[18,4,8,128]{3,2,1,0:T(8,128)} %param.5) | copy-start | bytes 884740
  18.4 9.9 %copy-start.3 = (s32[1,256]{1,0:T(1,128)S(1)}, s32[1,256]{1,0:T(1,128)}, u32[]{:S(2)}) copy-start(s32[1,256]{1,0:T(1,128)} %param.8) | copy-start | bytes 3076
  18.4 9.9 %copy-start.2 = (f32[1024]{0:T(1024)S(1)}, f32[1024]{0:T(1024)}, u32[]{:S(2)}) copy-start(f32[1024]{0:T(1024)} %param.9) | copy-start | bytes 12292
  18.4 10.1 %copy-start.5 = (s32[4,8,128]{2,1,0:T(8,128)S(1)}, s32[4,8,128]{2,1,0:T(8,128)}, u32[]{:S(2)}) copy-start(s32[4,8,128]{2,1,0:T(8,128)} %param.7) | copy-start | bytes 49156
  131.4 12.2 %copy-start.1 = (f32[4,8,128]{2,1,0:T(8,128)}, f32[4,8,128]{2,1,0:T(8,128)S(1)}, u32[]{:S(2)}) copy-start(f32[4,8,128]{2,1,0:T(8,128)S(1)} %get-tuple-element.19) | copy-start | bytes 49156
  131.5 7.5 %collective-permute-start.3 = (f32[1,8,128]{2,1,0:T(8,128)S(1)}, f32[1,8,128]{2,1,0:T(8,128)S(1)}, u32[]{:S(2)}, u32[]{:S(2)}) collective-permute-start(f32[1,8,128]{2,1,0:T(8,128)S(1)} %get-tuple-element.17), channel_id=1, source_target_pairs={{0,1},{1,2},{2,3},{3,4},{4,5},{5,6},{6,7},{7,8},{8,9},{9,10},{10,1... | collective-permute-start | bytes 12296 | tf_op jit(solution)/shard_map/ppermute | solution.py:29
  136.7 6.7 %collective-permute-start.2 = (f32[1,8,128]{2,1,0:T(8,128)S(1)}, f32[1,8,128]{2,1,0:T(8,128)S(1)}, u32[]{:S(2)}, u32[]{:S(2)}) collective-permute-start(f32[1,8,128]{2,1,0:T(8,128)S(1)} %get-tuple-element.16), channel_id=1, source_target_pairs={{1,0},{2,1},{3,2},{4,3},{5,4},{6,5},{7,6},{8,7},{9,8},{10,9},{11,1... | collective-permute-start | bytes 12296 | tf_op jit(solution)/shard_map/ppermute | solution.py:31
  143.6 0.7 copy-start.4

commit v2 on v1

v2 whole, which is shorter than its diff:
```python
import functools
import math

import jax
import jax.numpy as jnp
from jax import lax
from jax.experimental import pallas as pl
from jax.experimental.pallas import tpu as pltpu
from jax.sharding import PartitionSpec as P

LMAX = 40
HARM = 1681
NB = 1024


MESH = pl.DeviceIdType.MESH

time_step = 0.05


def padded_2(cells, sides, width):
    for axis, dim in sides:
        count = lax.axis_size(axis)
        ends = count - 1
        head = lax.slice_in_dim(cells, 0, width, axis=dim)
        tail = lax.slice_in_dim(cells, cells.shape[dim] - width, cells.shape[dim], axis=dim)
        cells = jnp.concatenate(
            [
                lax.ppermute(tail, axis, [(i, (i + 1) % count) for i in range(ends)]),
                cells,
                lax.ppermute(head, axis, [((i + 1) % count, i) for i in range(ends)]),
            ],
            axis=dim,
        )
    return cells


def degrees(harm_count):
    numbers = jnp.arange(harm_count, dtype=jnp.int32)
    marks = jnp.arange(1, LMAX + 1, dtype=jnp.int32) ** 2
    return jnp.sum((numbers[:, None] >= marks[None, :]).astype(jnp.int32), axis=1).astype(
        jnp.float32
    )


def log_steps(radius):
    bin_count = radius.shape[0]
    step_in = jnp.concatenate(
        [jnp.zeros((1,), radius.dtype), jnp.log(radius[:-1]) - jnp.log(radius[1:])]
    )
    step_out = jnp.concatenate([step_in[1:], jnp.zeros((1,), radius.dtype)])
    last_row = jnp.arange(bin_count, dtype=jnp.int32) == bin_count - 1
    return (step_in, step_out, last_row)


def round_up(value, step):
    return -(-value // step) * step


def one_hot(bin_row, row_total, listed):
    rows = lax.broadcasted_iota(jnp.int32, (row_total, listed), 0)
    return jnp.where(rows == bin_row, 1.0, 0.0).astype(jnp.bfloat16)


INNER = 8


def exchange_kernel(
    outer, part_ref, small_ref, grow_in_ref, grow_out_ref, radius_ref,
    shell_ref, extreme_ref,
    got, smalls, marks, sum_out, sum_in, dense, sent_back, came_back, worst,
    small_send, small_recv, part_send, part_recv, sum_send, sum_recv,
    worst_send, worst_recv, dense_send, dense_recv, back_send, back_recv,
):
    me = lax.axis_index("bricks")
    place, layer = lax.rem(me, INNER), me // INNER
    block, listed = part_ref.shape[2:]
    rows = radius_ref.shape[1]
    back_rows = dense.shape[1]

    def beside(offset):
        return lax.rem(place + offset, INNER)

    def above(offset):
        return lax.rem(layer + offset, outer)

    def in_layer(spot):
        return (layer * INNER + spot,)

    def in_column(level):
        return (level * INNER + place,)

    barrier = pltpu.get_barrier_semaphore()

    def greet_layer(offset, carry):
        pl.semaphore_signal(
            barrier, inc=1, device_id=in_layer(beside(offset)), device_id_type=MESH)
        return carry

    def greet_column(offset, carry):
        pl.semaphore_signal(
            barrier, inc=1, device_id=in_column(above(offset)), device_id_type=MESH)
        return carry

    lax.fori_loop(1, INNER, greet_layer, 0)
    lax.fori_loop(1, outer, greet_column, 0)
    smalls[place] = small_ref[...]
    got[place] = part_ref[place]
    pl.semaphore_wait(barrier, INNER + outer - 2)

    def small_copy(spot, slot):
        return pltpu.make_async_remote_copy(
            src_ref=small_ref, dst_ref=smalls.at[slot], send_sem=small_send.at[spot],
            recv_sem=small_recv.at[slot], device_id=in_layer(spot), device_id_type=MESH)

    def part_copy(spot, slot, level):
        return pltpu.make_async_remote_copy(
            src_ref=part_ref.at[spot, level], dst_ref=got.at[slot, level],
            send_sem=part_send.at[spot, level], recv_sem=part_recv.at[slot, level],
            device_id=in_layer(spot), device_id_type=MESH)

    def sum_copy(level, slot):
        return pltpu.make_async_remote_copy(
            src_ref=sum_out.at[level], dst_ref=sum_in.at[slot], send_sem=sum_send.at[level],
            recv_sem=sum_recv.at[slot], device_id=in_column(level), device_id_type=MESH)

    def worst_copy(level, slot):
        return pltpu.make_async_remote_copy(
            src_ref=worst.at[layer], dst_ref=worst.at[slot], send_sem=worst_send.at[level],
            recv_sem=worst_recv.at[slot], device_id=in_column(level), device_id_type=MESH)

    def dense_copy(level, slot):
        return pltpu.make_async_remote_copy(
            src_ref=dense.at[layer], dst_ref=dense.at[slot], send_sem=dense_send.at[level],
            recv_sem=dense_recv.at[slot], device_id=in_column(level), device_id_type=MESH)

    def back_copy(spot, slot, level):
        return pltpu.make_async_remote_copy(
            src_ref=sent_back.at[spot, level], dst_ref=came_back.at[slot, level],
            send_sem=back_send.at[spot, level], recv_sem=back_recv.at[slot, level],
            device_id=in_layer(spot), device_id_type=MESH)

    def send_small(offset, carry):
        small_copy(beside(offset), place).start()
        return carry

    lax.fori_loop(1, INNER, send_small, 0)

    def send_chunk(turn, carry):
        def send(offset, carry):
            part_copy(beside(offset), place, above(turn)).start()
            return carry

        return lax.fori_loop(1, INNER, send, carry)

    lax.fori_loop(1, outer + 1, send_chunk, 0)

    def columns(spot):
        return pl.ds(pl.multiple_of(spot * listed, listed), listed)

    def mark(spot):
        marks[:, columns(spot)] = one_hot(smalls[spot, 0:1, :].astype(jnp.int32), rows, listed)

    mark(place)

    def mark_other(offset, carry):
        spot = beside(INNER - offset)
        small_copy(beside(offset), spot).wait_recv()
        mark(spot)
        return carry

    lax.fori_loop(1, INNER, mark_other, 0)
    worst[layer] = jnp.max(smalls[...], axis=0)

    def send_worst(offset, carry):
        worst_copy(above(offset), layer).start()
        return carry

    lax.fori_loop(1, outer, send_worst, 0)

    def add_chunk(turn, carry):
        level = above(turn)

        def arrive(offset, carry):
            part_copy(beside(offset), beside(INNER - offset), level).wait_recv()
            return carry

        lax.fori_loop(1, INNER, arrive, 0)
        halves = []
        for spot in range(INNER):
            values = got[spot, level]
            high = values.astype(jnp.bfloat16).astype(jnp.float32)
            gap = jnp.zeros((64 - block, listed), jnp.float32)
            halves.append(
                jnp.concatenate([high, gap, values - high, gap], axis=0).astype(jnp.bfloat16)
            )
        both = lax.dot_general(
            marks[...], jnp.concatenate(halves, axis=1),
            (((1,), (1,)), ((), ())), preferred_element_type=jnp.float32)
        sum_out[level] = (both + pltpu.roll(both, 64, 1)).T[0:block]

        @pl.when(turn < outer)
        def _():
            sum_copy(level, layer).start()

        return carry

    lax.fori_loop(1, outer + 1, add_chunk, 0)
    sum_in[layer] = sum_out[layer]

    def sum_arrives(offset, carry):
        sum_copy(above(offset), above(outer - offset)).wait_recv()
        return carry

    lax.fori_loop(1, outer, sum_arrives, 0)
    scaled = jnp.sum(sum_in[...], axis=0) / radius_ref[...]
    field = -scaled
    for grow_ref, backward in ((grow_in_ref, False), (grow_out_ref, True)):
        factor, value = grow_ref[...], scaled
        step = 1
        while step < rows:
            turn = rows - step if backward else step
            value = value + factor * pltpu.roll(value, turn, 1)
            factor = factor * pltpu.roll(factor, turn, 1)
            step *= 2
        field = field + value
    if back_rows > block:
        field = jnp.concatenate(
            [field, jnp.zeros((back_rows - block, rows), jnp.float32)], axis=0)
    dense[layer] = field.astype(jnp.bfloat16)

    def send_dense(offset, carry):
        dense_copy(above(offset), layer).start()
        return carry

    lax.fori_loop(1, outer, send_dense, 0)

    def select(spot, level):
        return jnp.dot(
            dense[level], marks[:, columns(spot)], preferred_element_type=jnp.float32
        ).astype(jnp.bfloat16)

    def give_back(turn, carry):
        level = above(outer - turn)

        @pl.when(turn > 0)
        def _():
            dense_copy(above(turn), level).wait_recv()

        def give(offset, carry):
            spot = beside(offset)
            sent_back[spot, level] = select(spot, level)
            back_copy(spot, place, level).start()
            return carry

        lax.fori_loop(1, INNER, give, 0)
        came_back[place, level] = select(place, level)
        return carry

    lax.fori_loop(0, outer, give_back, 0)

    def finish_column(offset, carry):
        level, origin = above(offset), above(outer - offset)
        sum_copy(level, layer).wait_send()
        worst_copy(level, layer).wait_send()
        dense_copy(level, layer).wait_send()
        worst_copy(level, origin).wait_recv()
        return carry

    lax.fori_loop(1, outer, finish_column, 0)
    extreme_ref[...] = jnp.max(worst[...], axis=0)

    def finish_layer(offset, carry):
        spot, origin = beside(offset), beside(INNER - offset)
        small_copy(spot, place).wait_send()

        def finish(level, carry):
            part_copy(spot, place, level).wait_send()
            back_copy(spot, place, level).wait_send()
            back_copy(spot, origin, level).wait_recv()
            return carry

        return lax.fori_loop(0, outer, finish, carry)

    lax.fori_loop(1, INNER, finish_layer, 0)
    shell_ref[...] = came_back[...]


def exchange(parts, small, grow_in, grow_out, radius):
    inner, outer, block, listed = parts.shape
    rows = radius.shape[1]
    back_rows = round_up(block, 16)
    whole = pl.BlockSpec(memory_space=pltpu.VMEM)
    dma = pltpu.SemaphoreType.DMA
    return pl.pallas_call(
        functools.partial(exchange_kernel, outer),
        out_shape=(
            jax.ShapeDtypeStruct((inner, outer, back_rows, listed), jnp.bfloat16),
            jax.ShapeDtypeStruct(small.shape, jnp.float32),
        ),
        in_specs=[whole] * 5,
        out_specs=(whole, whole),
        scratch_shapes=[
            pltpu.VMEM(parts.shape, jnp.float32),
            pltpu.VMEM((inner,) + small.shape, jnp.float32),
            pltpu.VMEM((rows, inner * listed), jnp.bfloat16),
            pltpu.VMEM((outer, block, rows), jnp.float32),
            pltpu.VMEM((outer, block, rows), jnp.float32),
            pltpu.VMEM((outer, back_rows, rows), jnp.bfloat16),
            pltpu.VMEM((inner, outer, back_rows, listed), jnp.bfloat16),
            pltpu.VMEM((inner, outer, back_rows, listed), jnp.bfloat16),
            pltpu.VMEM((outer,) + small.shape, jnp.float32),
            dma((inner,)), dma((inner,)), dma((inner, outer)), dma((inner, outer)),
            dma((outer,)), dma((outer,)), dma((outer,)), dma((outer,)),
            dma((outer,)), dma((outer,)), dma((inner, outer)), dma((inner, outer)),
        ],
        compiler_params=pltpu.CompilerParams(
            collective_id=0, has_side_effects=True, vmem_limit_bytes=48 * 1024 * 1024
        ),
    )(parts, small, grow_in, grow_out, radius)


def advance(fluid_state, padded, potential_padded, lower_bound, upper_bound):
    channels = fluid_state.shape[0]
    speed = padded[channels]
    fields = padded[:channels]
    face_flux = 0.25 * (speed[1:] + speed[:-1])[None] * (fields[:, 1:] + fields[:, :-1])
    advanced = fluid_state - time_step * (face_flux[:, 1:] - face_flux[:, :-1])
    gradient = 0.5 * (potential_padded[2:] - potential_padded[:-2])
    density = advanced[0]
    momentum = advanced[1] - time_step * fluid_state[0] * gradient
    energy = advanced[4] - time_step * fluid_state[1] * gradient
    fraction = jnp.clip(
        advanced[5:] / density[None],
        lower_bound[:, None, None, None],
        upper_bound[:, None, None, None],
    )
    return jnp.concatenate(
        [density[None], momentum[None], advanced[2:4], energy[None], density[None] * fraction],
        axis=0,
    )


def per_device(fluid_state, harmonics, zone_slot, bin_list, shell_radius):
    channels, width_x, width_y, width_z = fluid_state.shape
    harm_count = harmonics.shape[0]
    zone_count = width_x * width_y * width_z
    device_count = lax.axis_size("bricks")
    flat_harm = harmonics.reshape(harm_count, zone_count)
    slot_flat = zone_slot.reshape(zone_count)
    my_bins = bin_list[0]
    listed = my_bins.shape[0]
    velocity = fluid_state[1] / fluid_state[0]
    extended = jnp.concatenate([fluid_state, velocity[None]], axis=0)
    padded = padded_2(extended.astype(jnp.bfloat16), (("bricks", 1),), 1).astype(extended.dtype)
    fractions = fluid_state[5:] / fluid_state[0][None]
    local_low = jnp.min(fractions, axis=(1, 2, 3))
    local_high = jnp.max(fractions, axis=(1, 2, 3))
    mass = fluid_state[0].reshape(zone_count).astype(jnp.bfloat16)
    selector = jnp.arange(listed, dtype=jnp.int32)[:, None] == slot_flat[None, :]
    weights = jnp.where(selector, mass[None, :], jnp.zeros((), jnp.bfloat16))
    partial_value = lax.dot_general(
        flat_harm, weights, (((1,), (1,)), ((), ())), preferred_element_type=jnp.float32
    )
    block = round_up(-(-harm_count // device_count), 8)
    outer = device_count // INNER
    me = lax.axis_index("bricks")
    own_block = lax.rem(me, INNER) * outer + me // INNER
    padded_count = block * device_count
    parts = jnp.pad(partial_value, ((0, padded_count - harm_count), (0, 0))).reshape(
        INNER, outer, block, listed
    )
    species = local_low.shape[0]
    extreme_row = jnp.pad(jnp.concatenate([-local_low, local_high]), (0, listed - 2 * species))
    small = jnp.pad(
        jnp.stack([my_bins.astype(jnp.float32), extreme_row]), ((0, 6), (0, 0))
    )
    own_degree = lax.dynamic_slice_in_dim(
        jnp.pad(degrees(harm_count), (0, padded_count - harm_count)), own_block * block, block)
    step_in, step_out, last_row = log_steps(shell_radius)
    first = jnp.arange(NB, dtype=jnp.int32) == 0
    grow_in = jnp.where(first[None, :], 0.0, jnp.exp((own_degree[:, None] + 1.0) * step_in[None, :]))
    grow_out = jnp.where(last_row[None, :], 0.0, jnp.exp(own_degree[:, None] * step_out[None, :]))
    radius = shell_radius[None, :]
    shells, extremes = exchange(parts, small, grow_in, grow_out, radius)
    lower_bound = -extremes[1, :species]
    upper_bound = extremes[1, species : 2 * species]
    shell_mine = shells[:, :, :block].reshape(padded_count, listed)[:harm_count].T
    product = jnp.dot(shell_mine, flat_harm, preferred_element_type=jnp.float32)
    factor = -1.0 / math.sqrt(float(HARM * zone_count * device_count))
    potential = (jnp.sum(jnp.where(selector, product, 0.0), axis=0) * factor).reshape(
        width_x, width_y, width_z
    )
    potential_padded = padded_2(potential, (("bricks", 0),), 1)
    new_state = advance(fluid_state, padded, potential_padded, lower_bound, upper_bound)
    return (new_state, potential)


def solution(mesh):
    placed = (
        P(None, "bricks", None, None),
        P(None, "bricks", None, None),
        P("bricks", None, None),
        P("bricks", None),
        P(),
    )
    return jax.shard_map(
        per_device,
        mesh=mesh,
        in_specs=placed,
        out_specs=(P(None, "bricks", None, None), P("bricks", None, None)),
        check_vma=False,
    )
```

time: 146 us -> 115 us (0.79); the launches traced: 144 us -> 115 us
  Pallas kernels: 84.9 us -> 53.7 us
    pallas_call x1, Pallas kernels: 84.9 us -> 53.7 us  [exchange(): pl.pallas_call(functools.partial(exchange_kernel, outer), out_shape=(jax....]
    unnamed x15 -> x13, local copies, waits for them, and re-layouts: 18.3 us -> 18.2 us
  transfers between devices with their start and end apart: 4 -> 4, of which waited for: 1 -> 1; matrix products, arithmetic and copies ran while one was open for 26% -> 0% of each run, Pallas kernels for 59% -> 0%
where the time goes in v2:
time: 115 us
  Pallas kernels  53.7 us (47%)
  local copies, waits for them, and re-layouts  19.2 us (17%)
  matrix products  16.8 us (15%)
  starting transfers between devices  14.9 us (13%)
  waiting for transfers between devices  5.1 us (4%)
  other arithmetic  4.3 us (4%)
    pallas_call x1, Pallas kernels, exchange(): pl.pallas_call(functools.partial(exchange_kernel, outer), out_shape=(jax....  53.7 us
    unnamed x13, local copies, waits for them, and re-layouts  18.2 us
    ppermute x2, starting transfers between devices, padded_2(): lax.ppermute(tail, axis, [(i, (i + 1) % count) for i in range(ends)])  10.6 us
    dot_general x1, matrix products, per_device(): product = jnp.dot(shell_mine, flat_harm, preferred_element_type=jnp.float32)  9.7 us
    dot_general x1, matrix products, per_device(): lax.dot_general(flat_harm, weights, (((1,), (1,)), ((), ())), preferred_e...  7.1 us
    ppermute x2, waiting for transfers between devices, padded_2(): lax.ppermute(head, axis, [((i + 1) % count, i) for i in range(ends)])  5.1 us
    ppermute x2, starting transfers between devices, padded_2(): lax.ppermute(head, axis, [((i + 1) % count, i) for i in range(ends)])  4.22 us
  transfers between devices with their start and end apart: 4, of which 1 were waited for; matrix products, arithmetic and copies ran while one was open for 0% of the time, Pallas kernels for 0%

profile of v2, /device:TPU:15, one launch (start us, length us, event | category | flops | bytes accessed | tf_op | source)
XLA Modules:
  0.0 114.8 jit_solution(6917542815727413118)
XLA Ops:
  0.7 0.7 slice_bitcast_fusion.3
  1.4 0.7 fusion.26
  2.1 0.1 convert_reduce_fusion
  2.3 0.8 log_subtract_fusion
  3.1 1.1 fusion.15
  4.2 0.7 convert_element_type.35
  4.9 7.8 %pad.58 = bf16[1688,32,128]{2,1,0:T(8,128)(2,1)S(1)} pad(bf16[1681,32,128]{2,1,0:T(8,128)(2,1)} %bitcast.66, bf16[]{:T(256)} %constant.22.clone.1), padding=0_7x0_0x0_0 | pad | bytes 27598850
  12.8 0.0 copy-start.4
  12.8 9.7 %copy.7 = bf16[211,8,32,128]{3,1,2,0:T(8,128)(2,1)} copy(bf16[211,8,32,128]{3,2,1,0:T(8,128)(2,1)S(1)} %bitcast.63) | data formatting | bytes 27656192
  22.4 0.1 broadcast_add_fusion
  22.5 0.1 pad_maximum_fusion.5
  22.6 0.1 select_maximum_fusion.1
  22.7 0.0 copy-done.4
  22.7 0.0 copy-start
  22.7 7.1 %convolution_bitcast_fusion = f32[1681,256]{1,0:T(8,128)S(1)} fusion(bf16[1681,4096]{1,0:T(8,128)(2,1)} %bitcast.64, s32[4096]{0:T(1024)S(1)} %bitcast.69, bf16[4096]{0:T(1024)(128)(2,1)S(1)} %fusion.26), kind=kOutput, calls=%fused_computation.3 | convolution fusion | flops 3527409664 | bytes 15516672 | tf_op jit(solution)/shard_map/dot_general | solution.py:362
  29.8 0.1 pad.16
  29.9 0.1 exponential_select_fusion
  30.1 0.0 copy-done
  30.1 53.7 %shard_map.68 = (bf16[8,4,64,256]{3,2,1,0:T(8,128)(2,1)S(1)}, f32[8,256]{1,0:T(8,128)S(1)}) custom-call(f32[8,4,56,256]{3,2,1,0:T(8,128)S(1)} %bitcast.61, f32[8,256]{1,0:T(8,128)S(1)} %select_maximum_fusion.small_ref, f32[56,1024]{1,0:T(8,128)S(1)} %get-tuple-element.25.grow_in_ref, f32[56,1024]{1,0:T(8,128)S(1)} %get-tuple-element.24.grow_out_ref, ...), custom_call_target="tpu_custom_call" | custom-call | tf_op jit(solution)/shard_map/pallas_call | solution.py:295
  83.8 0.1 slice.117
  83.9 0.0 copy-start.1
  83.9 9.7 %fusion.3 = f32[4096]{0:T(1024)S(1)} fusion(bf16[1681,4096]{1,0:T(8,128)(2,1)} %bitcast.65, s32[4096]{0:T(1024)S(1)} %bitcast.70, bf16[1792,256]{1,0:T(8,128)(2,1)S(1)} %bitcast.67), kind=kOutput, calls=%fused_computation.5 | convolution fusion | flops 3528454144 | bytes 14667776 | tf_op jit(solution)/shard_map/dot_general | solution.py:389
  93.6 0.0 copy-start.2
  93.6 2.3 %collective-permute-start.2 = (f32[1,8,128]{2,1,0:T(8,128)S(1)}, f32[1,8,128]{2,1,0:T(8,128)S(1)}, u32[]{:S(2)}, u32[]{:S(2)}) collective-permute-start(f32[1,8,128]{2,1,0:T(8,128)S(1)} %get-tuple-element.16), channel_id=1, source_target_pairs={{1,0},{2,1},{3,2},{4,3},{5,4},{6,5},{7,6},{8,7},{9,8},{10,9},{11,1... | collective-permute-start | bytes 12296 | tf_op jit(solution)/shard_map/ppermute | solution.py:31
  95.9 8.2 %collective-permute-start.3 = (f32[1,8,128]{2,1,0:T(8,128)S(1)}, f32[1,8,128]{2,1,0:T(8,128)S(1)}, u32[]{:S(2)}, u32[]{:S(2)}) collective-permute-start(f32[1,8,128]{2,1,0:T(8,128)S(1)} %get-tuple-element.17), channel_id=1, source_target_pairs={{0,1},{1,2},{2,3},{3,4},{4,5},{5,6},{6,7},{7,8},{8,9},{9,10},{10,1... | collective-permute-start | bytes 12296 | tf_op jit(solution)/shard_map/ppermute | solution.py:29
  104.2 0.0 copy-done.1
  104.2 2.4 %collective-permute-start = (bf16[19,1,8,128]{3,2,1,0:T(8,128)(2,1)S(1)}, bf16[19,1,8,128]{3,2,1,0:T(8,128)(2,1)S(1)}, u32[]{:S(2)}, u32[]{:S(2)}) collective-permute-start(bf16[19,1,8,128]{3,2,1,0:T(8,128)(2,1)S(1)} %get-tuple-element.14), channel_id=1, source_target_pairs={{0,1},{1,2},{2,3},{3,4},{4,5},{5,6},{6,7},{7,8},{8,9},{9,10},{10,1... | collective-permute-start | bytes 116744 | tf_op jit(solution)/shard_map/ppermute | solution.py:29
  106.6 1.9 %collective-permute-start.1 = (bf16[19,1,8,128]{3,2,1,0:T(8,128)(2,1)S(1)}, bf16[19,1,8,128]{3,2,1,0:T(8,128)(2,1)S(1)}, u32[]{:S(2)}, u32[]{:S(2)}) collective-permute-start(bf16[19,1,8,128]{3,2,1,0:T(8,128)(2,1)S(1)} %get-tuple-element.15), channel_id=1, source_target_pairs={{1,0},{2,1},{3,2},{4,3},{5,4},{6,5},{7,6},{8,7},{9,8},{10,9},{11,1... | collective-permute-start | bytes 116744 | tf_op jit(solution)/shard_map/ppermute | solution.py:31
  108.6 0.1 slice_bitcast_fusion.6
  108.6 0.0 collective-permute-done
  108.6 5.1 %collective-permute-done.1 = bf16[19,1,8,128]{3,2,1,0:T(8,128)(2,1)S(1)} collective-permute-done((bf16[19,1,8,128]{3,2,1,0:T(8,128)(2,1)S(1)}, bf16[19,1,8,128]{3,2,1,0:T(8,128)(2,1)S(1)}, u32[]{:S(2)}, u32[]{:S(2)}) %collective-permute-start.1) | collective-permute-done | bytes 38944 | tf_op jit(solution)/shard_map/ppermute | solution.py:31
  113.7 0.1 maximum_convert_fusion
  113.8 0.1 fusion.9
  113.9 0.0 collective-permute-done.2
  113.9 0.0 collective-permute-done.3
  114.0 0.1 fusion.13
  114.1 0.0 copy-done.2
  114.1 0.0 copy-start.3
  114.1 0.7 copy-done.3
  (16 shorter events, 0.2 us)
Async XLA Ops:
  12.8 9.9 %copy-start.4 = (s32[4,8,128]{2,1,0:T(8,128)S(1)}, s32[4,8,128]{2,1,0:T(8,128)}, u32[]{:S(2)}) copy-start(s32[4,8,128]{2,1,0:T(8,128)} %param.7) | copy-start | bytes 49156
  22.7 7.4 %copy-start = (f32[1024]{0:T(1024)S(1)}, f32[1024]{0:T(1024)}, u32[]{:S(2)}) copy-start(f32[1024]{0:T(1024)} %param.9) | copy-start | bytes 12292
  83.9 20.3 %copy-start.1 = (f32[18,4,8,128]{3,2,1,0:T(8,128)S(1)}, f32[18,4,8,128]{3,2,1,0:T(8,128)}, u32[]{:S(2)}) copy-start(f32[18,4,8,128]{3,2,1,0:T(8,128)} %param.5) | copy-start | bytes 884740
  93.6 20.5 %copy-start.2 = (f32[4,8,128]{2,1,0:T(8,128)}, f32[4,8,128]{2,1,0:T(8,128)S(1)}, u32[]{:S(2)}) copy-start(f32[4,8,128]{2,1,0:T(8,128)S(1)} %get-tuple-element.19) | copy-start | bytes 49156
  93.6 20.3 %collective-permute-start.2 = (f32[1,8,128]{2,1,0:T(8,128)S(1)}, f32[1,8,128]{2,1,0:T(8,128)S(1)}, u32[]{:S(2)}, u32[]{:S(2)}) collective-permute-start(f32[1,8,128]{2,1,0:T(8,128)S(1)} %get-tuple-element.16), channel_id=1, source_target_pairs={{1,0},{2,1},{3,2},{4,3},{5,4},{6,5},{7,6},{8,7},{9,8},{10,9},{11,1... | collective-permute-start | bytes 12296 | tf_op jit(solution)/shard_map/ppermute | solution.py:31
  95.9 18.0 %collective-permute-start.3 = (f32[1,8,128]{2,1,0:T(8,128)S(1)}, f32[1,8,128]{2,1,0:T(8,128)S(1)}, u32[]{:S(2)}, u32[]{:S(2)}) collective-permute-start(f32[1,8,128]{2,1,0:T(8,128)S(1)} %get-tuple-element.17), channel_id=1, source_target_pairs={{0,1},{1,2},{2,3},{3,4},{4,5},{5,6},{6,7},{7,8},{8,9},{9,10},{10,1... | collective-permute-start | bytes 12296 | tf_op jit(solution)/shard_map/ppermute | solution.py:29
  104.2 4.4 %collective-permute-start = (bf16[19,1,8,128]{3,2,1,0:T(8,128)(2,1)S(1)}, bf16[19,1,8,128]{3,2,1,0:T(8,128)(2,1)S(1)}, u32[]{:S(2)}, u32[]{:S(2)}) collective-permute-start(bf16[19,1,8,128]{3,2,1,0:T(8,128)(2,1)S(1)} %get-tuple-element.14), channel_id=1, source_target_pairs={{0,1},{1,2},{2,3},{3,4},{4,5},{5,6},{6,7},{7,8},{8,9},{9,10},{10,1... | collective-permute-start | bytes 116744 | tf_op jit(solution)/shard_map/ppermute | solution.py:29
  106.6 7.1 %collective-permute-start.1 = (bf16[19,1,8,128]{3,2,1,0:T(8,128)(2,1)S(1)}, bf16[19,1,8,128]{3,2,1,0:T(8,128)(2,1)S(1)}, u32[]{:S(2)}, u32[]{:S(2)}) collective-permute-start(bf16[19,1,8,128]{3,2,1,0:T(8,128)(2,1)S(1)} %get-tuple-element.15), channel_id=1, source_target_pairs={{1,0},{2,1},{3,2},{4,3},{5,4},{6,5},{7,6},{8,7},{9,8},{10,9},{11,1... | collective-permute-start | bytes 116744 | tf_op jit(solution)/shard_map/ppermute | solution.py:31
  114.1 0.7 copy-start.3

commit v3 on v2

--- a/solution.py
+++ b/solution.py
@@ -66,11 +66,12 @@
 
 
 def exchange_kernel(
-    outer, part_ref, small_ref, grow_in_ref, grow_out_ref, radius_ref,
-    shell_ref, extreme_ref,
-    got, smalls, marks, sum_out, sum_in, dense, sent_back, came_back, worst,
+    outer, part_ref, small_ref, grow_in_ref, grow_out_ref, radius_ref, edge_ref,
+    shell_ref, extreme_ref, halo_ref,
+    got, smalls, marks, sum_out, sum_in, dense, sent_back, came_back, worst, halo,
     small_send, small_recv, part_send, part_recv, sum_send, sum_recv,
     worst_send, worst_recv, dense_send, dense_recv, back_send, back_recv,
+    edge_send, edge_recv,
 ):
     me = lax.axis_index("bricks")
     place, layer = lax.rem(me, INNER), me // INNER
@@ -102,11 +103,15 @@
             barrier, inc=1, device_id=in_column(above(offset)), device_id_type=MESH)
         return carry
 
+    count = outer * INNER
+    ring = ((lax.rem(me + count - 1, count),), (lax.rem(me + 1, count),))
+    for neighbour in ring:
+        pl.semaphore_signal(barrier, inc=1, device_id=neighbour, device_id_type=MESH)
     lax.fori_loop(1, INNER, greet_layer, 0)
     lax.fori_loop(1, outer, greet_column, 0)
     smalls[place] = small_ref[...]
     got[place] = part_ref[place]
-    pl.semaphore_wait(barrier, INNER + outer - 2)
+    pl.semaphore_wait(barrier, INNER + outer)
 
     def small_copy(spot, slot):
         return pltpu.make_async_remote_copy(
@@ -139,6 +144,13 @@
             src_ref=sent_back.at[spot, level], dst_ref=came_back.at[slot, level],
             send_sem=back_send.at[spot, level], recv_sem=back_recv.at[slot, level],
             device_id=in_layer(spot), device_id_type=MESH)
+
+    edges = [
+        pltpu.make_async_remote_copy(
+            src_ref=edge_ref.at[side], dst_ref=halo.at[1 - side], send_sem=edge_send.at[side],
+            recv_sem=edge_recv.at[1 - side], device_id=ring[side], device_id_type=MESH)
+        for side in range(2)
+    ]
 
     def send_small(offset, carry):
         small_copy(beside(offset), place).start()
@@ -154,6 +166,9 @@
         return lax.fori_loop(1, INNER, send, carry)
 
     lax.fori_loop(1, outer + 1, send_chunk, 0)
+
+    for edge in edges:
+        edge.start()
 
     def columns(spot):
         return pl.ds(pl.multiple_of(spot * listed, listed), listed)
@@ -284,9 +299,12 @@
 
     lax.fori_loop(1, INNER, finish_layer, 0)
     shell_ref[...] = came_back[...]
-
-
-def exchange(parts, small, grow_in, grow_out, radius):
+    for edge in edges:
+        edge.wait()
+    halo_ref[...] = halo[...]
+
+
+def exchange(parts, small, grow_in, grow_out, radius, edges):
     inner, outer, block, listed = parts.shape
     rows = radius.shape[1]
     back_rows = round_up(block, 16)
@@ -297,9 +315,10 @@
         out_shape=(
             jax.ShapeDtypeStruct((inner, outer, back_rows, listed), jnp.bfloat16),
             jax.ShapeDtypeStruct(small.shape, jnp.float32),
+            jax.ShapeDtypeStruct(edges.shape, edges.dtype),
         ),
-        in_specs=[whole] * 5,
-        out_specs=(whole, whole),
+        in_specs=[whole] * 6,
+        out_specs=(whole, whole, whole),
         scratch_shapes=[
             pltpu.VMEM(parts.shape, jnp.float32),
             pltpu.VMEM((inner,) + small.shape, jnp.float32),
@@ -310,14 +329,51 @@
             pltpu.VMEM((inner, outer, back_rows, listed), jnp.bfloat16),
             pltpu.VMEM((inner, outer, back_rows, listed), jnp.bfloat16),
             pltpu.VMEM((outer,) + small.shape, jnp.float32),
+            pltpu.VMEM(edges.shape, edges.dtype),
             dma((inner,)), dma((inner,)), dma((inner, outer)), dma((inner, outer)),
             dma((outer,)), dma((outer,)), dma((outer,)), dma((outer,)),
             dma((outer,)), dma((outer,)), dma((inner, outer)), dma((inner, outer)),
+            dma((2,)), dma((2,)),
         ],
         compiler_params=pltpu.CompilerParams(
             collective_id=0, has_side_effects=True, vmem_limit_bytes=48 * 1024 * 1024
         ),
-    )(parts, small, grow_in, grow_out, radius)
+    )(parts, small, grow_in, grow_out, radius, edges)
+
+
+TILE = 224
+
+
+def moment_kernel(harm_count, harm_ref, weight_ref, flat_ref, part_ref):
+    tile, lines, width = harm_ref.shape
+    values = harm_ref[...].reshape(tile, lines * width)
+    flat_ref[...] = values
+    sums = jnp.dot(values, weight_ref[...], preferred_element_type=jnp.float32)
+    number = pl.program_id(0) * tile + lax.broadcasted_iota(jnp.int32, sums.shape, 0)
+    part_ref[...] = jnp.where(number < harm_count, sums, 0.0)
+
+
+def flat_and_moments(harm, weights):
+    harm_count, lines, width = harm.shape
+    zone_count, listed = weights.shape
+    steps = -(-harm_count // TILE)
+    return pl.pallas_call(
+        functools.partial(moment_kernel, harm_count),
+        grid=(steps,),
+        out_shape=(
+            jax.ShapeDtypeStruct((harm_count, zone_count), harm.dtype),
+            jax.ShapeDtypeStruct((steps * TILE, listed), jnp.float32),
+        ),
+        in_specs=[
+            pl.BlockSpec((TILE, lines, width), lambda i: (i, 0, 0)),
+            pl.BlockSpec((zone_count, listed), lambda i: (0, 0)),
+        ],
+        out_specs=(
+            pl.BlockSpec((TILE, zone_count), lambda i: (i, 0)),
+            pl.BlockSpec((TILE, listed), lambda i: (i, 0)),
+        ),
+        compiler_params=pltpu.CompilerParams(vmem_limit_bytes=48 * 1024 * 1024),
+    )(harm, weights)
 
 
 def advance(fluid_state, padded, potential_padded, lower_bound, upper_bound):
@@ -346,28 +402,32 @@
     harm_count = harmonics.shape[0]
     zone_count = width_x * width_y * width_z
     device_count = lax.axis_size("bricks")
-    flat_harm = harmonics.reshape(harm_count, zone_count)
     slot_flat = zone_slot.reshape(zone_count)
     my_bins = bin_list[0]
     listed = my_bins.shape[0]
     velocity = fluid_state[1] / fluid_state[0]
     extended = jnp.concatenate([fluid_state, velocity[None]], axis=0)
-    padded = padded_2(extended.astype(jnp.bfloat16), (("bricks", 1),), 1).astype(extended.dtype)
+    rounded = extended.astype(jnp.bfloat16)
+    edges = jnp.stack([rounded[:, 0], rounded[:, -1]]).reshape(2, -1, width_z)
+    line_count = edges.shape[1]
+    edges = jnp.pad(edges, ((0, 0), (0, -line_count % 16), (0, 0)))
     fractions = fluid_state[5:] / fluid_state[0][None]
     local_low = jnp.min(fractions, axis=(1, 2, 3))
     local_high = jnp.max(fractions, axis=(1, 2, 3))
     mass = fluid_state[0].reshape(zone_count).astype(jnp.bfloat16)
     selector = jnp.arange(listed, dtype=jnp.int32)[:, None] == slot_flat[None, :]
-    weights = jnp.where(selector, mass[None, :], jnp.zeros((), jnp.bfloat16))
-    partial_value = lax.dot_general(
-        flat_harm, weights, (((1,), (1,)), ((), ())), preferred_element_type=jnp.float32
-    )
+    weights = jnp.where(
+        slot_flat[:, None] == jnp.arange(listed, dtype=jnp.int32)[None, :],
+        mass[:, None], jnp.zeros((), jnp.bfloat16))
+    flat_harm, partial_value = flat_and_moments(
+        harmonics.reshape(harm_count, width_x * width_y, width_z), weights)
     block = round_up(-(-harm_count // device_count), 8)
     outer = device_count // INNER
     me = lax.axis_index("bricks")
     own_block = lax.rem(me, INNER) * outer + me // INNER
     padded_count = block * device_count
-    parts = jnp.pad(partial_value, ((0, padded_count - harm_count), (0, 0))).reshape(
+    spare = max(padded_count - partial_value.shape[0], 0)
+    parts = jnp.pad(partial_value, ((0, spare), (0, 0)))[:padded_count].reshape(
         INNER, outer, block, listed
     )
     species = local_low.shape[0]
@@ -382,7 +442,11 @@
     grow_in = jnp.where(first[None, :], 0.0, jnp.exp((own_degree[:, None] + 1.0) * step_in[None, :]))
     grow_out = jnp.where(last_row[None, :], 0.0, jnp.exp(own_degree[:, None] * step_out[None, :]))
     radius = shell_radius[None, :]
-    shells, extremes = exchange(parts, small, grow_in, grow_out, radius)
+    shells, extremes, halo = exchange(parts, small, grow_in, grow_out, radius, edges)
+    halo = halo[:, :line_count].reshape(2, channels + 1, 1, width_y, width_z)
+    below = jnp.where(me > 0, halo[0], jnp.zeros_like(halo[0]))
+    beyond = jnp.where(me < device_count - 1, halo[1], jnp.zeros_like(halo[1]))
+    padded = jnp.concatenate([below, rounded, beyond], axis=1).astype(extended.dtype)
     lower_bound = -extremes[1, :species]
     upper_bound = extremes[1, species : 2 * species]
     shell_mine = shells[:, :, :block].reshape(padded_count, listed)[:harm_count].T

time: 115 us -> 105 us (0.913)
  local copies, waits for them, and re-layouts: 19.2 us -> 1.55 us
  Pallas kernels: 53.7 us -> 69.1 us
  matrix products: 16.8 us -> 9.59 us
  starting transfers between devices: 14.9 us -> 10.8 us
  other arithmetic: 4.3 us -> 7.72 us
    unnamed x13 -> x11, local copies, waits for them, and re-layouts: 18.2 us -> 0.74 us
    pallas_call x0 -> x1, Pallas kernels: none -> 15.2 us  [flat_and_moments(): pl.pallas_call(functools.partial(moment_kernel, harm_count), grid=(steps,...]
    dot_general x1 -> x0, matrix products: 7.1 us -> none  [per_device(): lax.dot_general(flat_harm, weights, (((1,), (1,)), ((), ())), preferred_e...]
    select_n x0 -> x2, other arithmetic: none -> 2.46 us  [the longest x1 2.44 us: per_device(): jnp.where(slot_flat[:, None] == jnp.arange(listed, dtype=jnp.int32)[None,...]
    ppermute x2 -> x1, starting transfers between devices: 4.22 us -> 1.92 us  [padded_2(): lax.ppermute(head, axis, [((i + 1) % count, i) for i in range(ends)])]
    ppermute x2 -> x1, starting transfers between devices: 10.6 us -> 8.86 us  [padded_2(): lax.ppermute(tail, axis, [(i, (i + 1) % count) for i in range(ends)])]
    another operation x1 -> x4, other arithmetic: 0.02 us -> 1.74 us
    ppermute x2 -> x1, waiting for transfers between devices: 5.1 us -> 4.48 us  [padded_2(): lax.ppermute(head, axis, [((i + 1) % count, i) for i in range(ends)])]
  transfers between devices with their start and end apart: 4 -> 2, of which waited for: 1 -> 1; matrix products, arithmetic and copies ran while one was open for 0% -> 0% of each run, Pallas kernels for 0% -> 0%
where the time goes in v3:
time: 105 us; the launch traced here: 104 us
  Pallas kernels  69.1 us (66%)
  starting transfers between devices  10.8 us (10%)
  matrix products  9.59 us (9%)
  other arithmetic  7.72 us (7%)
  waiting for transfers between devices  4.48 us (4%)
  local copies, waits for them, and re-layouts  1.55 us (1%)
    pallas_call x1, Pallas kernels, exchange(): pl.pallas_call(functools.partial(exchange_kernel, outer), out_shape=(jax....  53.9 us
    pallas_call x1, Pallas kernels, flat_and_moments(): pl.pallas_call(functools.partial(moment_kernel, harm_count), grid=(steps,...  15.2 us
    dot_general x1, matrix products, per_device(): product = jnp.dot(shell_mine, flat_harm, preferred_element_type=jnp.float32)  9.59 us
    ppermute x1, starting transfers between devices, padded_2(): lax.ppermute(tail, axis, [(i, (i + 1) % count) for i in range(ends)])  8.86 us
    ppermute x1, waiting for transfers between devices, padded_2(): lax.ppermute(head, axis, [((i + 1) % count, i) for i in range(ends)])  4.48 us
    select_n x1, other arithmetic, per_device(): jnp.where(slot_flat[:, None] == jnp.arange(listed, dtype=jnp.int32)[None,...  2.44 us
  transfers between devices with their start and end apart: 2, of which 1 were waited for; matrix products, arithmetic and copies ran while one was open for 0% of the time, Pallas kernels for 0%

profile of v3, /device:TPU:15, one launch (start us, length us, event | category | flops | bytes accessed | tf_op | source)
XLA Modules:
  0.0 104.1 jit_solution(6177150639971781720)
XLA Ops:
  0.6 0.7 fusion.26
  1.4 0.7 divide_convert_fusion
  2.1 1.0 convert.6
  3.1 1.1 %fusion.14 = (f32[13]{0:T(128)S(1)}, f32[13]{0:T(128)S(1)}) fusion(f32[4,8,128]{2,1,0:T(8,128)S(1)} %get-tuple-element.19, f32[18,4,8,128]{3,2,1,0:T(8,128)} %param.5), kind=kLoop, calls=%fused_computation.27 | loop fusion | flops 159718 | bytes 229480 | tf_op jit(solution)/shard_map/reduce_min | solution.py:415
  4.2 0.7 convert_element_type.34
  4.9 0.8 log_subtract_fusion
  5.8 0.1 convert_reduce_fusion
  5.9 2.4 %fusion.weight_ref = bf16[4096,256]{1,0:T(8,128)(2,1)S(1)} fusion(s32[4096]{0:T(1024)} %bitcast.71, bf16[4096]{0:T(1024)(128)(2,1)S(1)} %fusion.26), kind=kLoop, calls=%fused_computation.3 | loop fusion | flops 2097152 | bytes 2121728 | tf_op jit(solution)/shard_map/jit(_where)/select_n | solution.py:419
  8.3 0.0 copy-start
  8.4 15.2 %shard_map.68 = (bf16[1681,4096]{1,0:T(8,128)(2,1)}, f32[1792,256]{1,0:T(8,128)S(1)}) custom-call(bf16[1681,32,128]{2,1,0:T(8,128)(2,1)} %bitcast.69, bf16[4096,256]{1,0:T(8,128)(2,1)S(1)} %fusion.weight_ref), custom_call_target="tpu_custom_call" | custom-call | tf_op jit(solution)/shard_map/pallas_call | solution.py:360
  23.6 0.0 copy-start.3
  23.6 0.1 select_maximum_fusion.1
  23.7 0.1 pad_maximum_fusion.4
  23.7 0.1 broadcast_add_fusion
  23.8 0.1 exponential_select_fusion
  24.0 0.0 copy-done
  24.0 53.9 %shard_map.69 = (bf16[8,4,64,256]{3,2,1,0:T(8,128)(2,1)S(1)}, f32[8,256]{1,0:T(8,128)S(1)}, bf16[2,160,128]{2,1,0:T(8,128)(2,1)S(1)}) custom-call(f32[8,4,56,256]{3,2,1,0:T(8,128)S(1)} %bitcast.67, f32[8,256]{1,0:T(8,128)S(1)} %select_maximum_fusion.small_ref, f32[56,1024]{1,0:T(8,128)S(1)} %get-tuple-element.33.grow_in_ref, ...), custom_call_target="tpu_custom_call" | custom-call | tf_op jit(solution)/shard_map/pallas_call | solution.py:313
  77.9 0.1 slice.130
  78.0 0.0 copy-done.3
  78.0 0.0 copy-start.1
  78.0 9.6 %fusion.1 = f32[4096]{0:T(1024)S(1)} fusion(bf16[1681,4096]{1,0:T(8,128)(2,1)} %get-tuple-element.10, s32[4096]{0:T(1024)S(1)} %bitcast.72, bf16[1792,256]{1,0:T(8,128)(2,1)S(1)} %bitcast.70), kind=kOutput, calls=%fused_computation.4 | convolution fusion | flops 3528454144 | bytes 14667776 | tf_op jit(solution)/shard_map/dot_general | solution.py:453
  87.6 0.0 copy-start.2
  87.7 8.9 %collective-permute-start.1 = (f32[1,8,128]{2,1,0:T(8,128)S(1)}, f32[1,8,128]{2,1,0:T(8,128)S(1)}, u32[]{:S(2)}, u32[]{:S(2)}) collective-permute-start(f32[1,8,128]{2,1,0:T(8,128)S(1)} %get-tuple-element.25), channel_id=1, source_target_pairs={{0,1},{1,2},{2,3},{3,4},{4,5},{5,6},{6,7},{7,8},{8,9},{9,10},{10,1... | collective-permute-start | bytes 12296 | tf_op jit(solution)/shard_map/ppermute | solution.py:29
  96.5 1.9 %collective-permute-start = (f32[1,8,128]{2,1,0:T(8,128)S(1)}, f32[1,8,128]{2,1,0:T(8,128)S(1)}, u32[]{:S(2)}, u32[]{:S(2)}) collective-permute-start(f32[1,8,128]{2,1,0:T(8,128)S(1)} %get-tuple-element.24), channel_id=1, source_target_pairs={{1,0},{2,1},{3,2},{4,3},{5,4},{6,5},{7,6},{8,7},{9,8},{10,9},{11,1... | collective-permute-start | bytes 12296 | tf_op jit(solution)/shard_map/ppermute | solution.py:31
  98.5 0.1 maximum_convert_fusion
  98.6 0.0 copy-done.1
  98.6 0.1 fusion.5
  98.7 0.1 slice_bitcast_fusion.6
  98.8 0.0 collective-permute-done.1
  98.8 4.5 %collective-permute-done = f32[1,8,128]{2,1,0:T(8,128)S(1)} collective-permute-done((f32[1,8,128]{2,1,0:T(8,128)S(1)}, f32[1,8,128]{2,1,0:T(8,128)S(1)}, u32[]{:S(2)}, u32[]{:S(2)}) %collective-permute-start) | collective-permute-done | bytes 4128 | tf_op jit(solution)/shard_map/ppermute | solution.py:31
  103.3 0.1 fusion.9
  103.4 0.0 copy-done.2
  103.4 0.0 copy-start.4
  103.4 0.7 copy-done.4
  (17 shorter events, 0.1 us)
Async XLA Ops:
  8.3 15.6 %copy-start = (f32[1024]{0:T(1024)S(1)}, f32[1024]{0:T(1024)}, u32[]{:S(2)}) copy-start(f32[1024]{0:T(1024)} %param.9) | copy-start | bytes 12292
  23.6 54.4 %copy-start.3 = (s32[4,8,128]{2,1,0:T(8,128)S(1)}, s32[4,8,128]{2,1,0:T(8,128)}, u32[]{:S(2)}) copy-start(s32[4,8,128]{2,1,0:T(8,128)} %param.7) | copy-start | bytes 49156
  78.0 20.6 %copy-start.1 = (f32[18,4,8,128]{3,2,1,0:T(8,128)S(1)}, f32[18,4,8,128]{3,2,1,0:T(8,128)}, u32[]{:S(2)}) copy-start(f32[18,4,8,128]{3,2,1,0:T(8,128)} %param.5) | copy-start | bytes 884740
  87.6 15.8 %copy-start.2 = (f32[4,8,128]{2,1,0:T(8,128)}, f32[4,8,128]{2,1,0:T(8,128)S(1)}, u32[]{:S(2)}) copy-start(f32[4,8,128]{2,1,0:T(8,128)S(1)} %get-tuple-element.27) | copy-start | bytes 49156
  87.7 11.1 %collective-permute-start.1 = (f32[1,8,128]{2,1,0:T(8,128)S(1)}, f32[1,8,128]{2,1,0:T(8,128)S(1)}, u32[]{:S(2)}, u32[]{:S(2)}) collective-permute-start(f32[1,8,128]{2,1,0:T(8,128)S(1)} %get-tuple-element.25), channel_id=1, source_target_pairs={{0,1},{1,2},{2,3},{3,4},{4,5},{5,6},{6,7},{7,8},{8,9},{9,10},{10,1... | collective-permute-start | bytes 12296 | tf_op jit(solution)/shard_map/ppermute | solution.py:29
  96.5 6.7 %collective-permute-start = (f32[1,8,128]{2,1,0:T(8,128)S(1)}, f32[1,8,128]{2,1,0:T(8,128)S(1)}, u32[]{:S(2)}, u32[]{:S(2)}) collective-permute-start(f32[1,8,128]{2,1,0:T(8,128)S(1)} %get-tuple-element.24), channel_id=1, source_target_pairs={{1,0},{2,1},{3,2},{4,3},{5,4},{6,5},{7,6},{8,7},{9,8},{10,9},{11,1... | collective-permute-start | bytes 12296 | tf_op jit(solution)/shard_map/ppermute | solution.py:31
  103.4 0.7 copy-start.4

commit v4 on v3

--- a/solution.py
+++ b/solution.py
@@ -336,7 +336,7 @@
             dma((2,)), dma((2,)),
         ],
         compiler_params=pltpu.CompilerParams(
-            collective_id=0, has_side_effects=True, vmem_limit_bytes=48 * 1024 * 1024
+            collective_id=0, has_side_effects=True, vmem_limit_bytes=28 * 1024 * 1024
         ),
     )(parts, small, grow_in, grow_out, radius, edges)
 
@@ -372,7 +372,7 @@
             pl.BlockSpec((TILE, zone_count), lambda i: (i, 0)),
             pl.BlockSpec((TILE, listed), lambda i: (i, 0)),
         ),
-        compiler_params=pltpu.CompilerParams(vmem_limit_bytes=48 * 1024 * 1024),
+        compiler_params=pltpu.CompilerParams(vmem_limit_bytes=28 * 1024 * 1024),
     )(harm, weights)
 
 

time: 105 us -> 104 us (level)
  Pallas kernels: 69.1 us -> 62.9 us
  local copies, waits for them, and re-layouts: 1.55 us -> 6.45 us
    pallas_call x1, Pallas kernels: 15.2 us -> 9 us  [flat_and_moments(): pl.pallas_call(functools.partial(moment_kernel, harm_count), grid=(steps,...]
    unnamed x11 -> x13, local copies, waits for them, and re-layouts: 0.74 us -> 5.64 us
where the time goes in v4:
time: 104 us; the launch traced here: 103 us
  Pallas kernels  62.9 us (60%)
  starting transfers between devices  10.8 us (10%)
  matrix products  9.63 us (9%)
  other arithmetic  7.71 us (7%)
  local copies, waits for them, and re-layouts  6.45 us (6%)
  waiting for transfers between devices  4.49 us (4%)
    pallas_call x1, Pallas kernels, exchange(): pl.pallas_call(functools.partial(exchange_kernel, outer), out_shape=(jax....  53.9 us
    dot_general x1, matrix products, per_device(): product = jnp.dot(shell_mine, flat_harm, preferred_element_type=jnp.float32)  9.63 us
    pallas_call x1, Pallas kernels, flat_and_moments(): pl.pallas_call(functools.partial(moment_kernel, harm_count), grid=(steps,...  9 us
    ppermute x1, starting transfers between devices, padded_2(): lax.ppermute(tail, axis, [(i, (i + 1) % count) for i in range(ends)])  8.87 us
    unnamed x13, local copies, waits for them, and re-layouts  5.64 us
    ppermute x1, waiting for transfers between devices, padded_2(): lax.ppermute(head, axis, [((i + 1) % count, i) for i in range(ends)])  4.48 us
    select_n x1, other arithmetic, per_device(): jnp.where(slot_flat[:, None] == jnp.arange(listed, dtype=jnp.int32)[None,...  2.44 us
  transfers between devices with their start and end apart: 2, of which 1 were waited for; matrix products, arithmetic and copies ran while one was open for 0% of the time, Pallas kernels for 0%

profile of v4, /device:TPU:15, one launch (start us, length us, event | category | flops | bytes accessed | tf_op | source)
XLA Modules:
  0.0 102.9 jit_solution(15073395781329201662)
XLA Ops:
  0.6 0.7 fusion.26
  1.4 0.7 divide_convert_fusion
  2.1 1.0 convert.6
  3.1 1.1 %fusion.14 = (f32[13]{0:T(128)S(1)}, f32[13]{0:T(128)S(1)}) fusion(f32[4,8,128]{2,1,0:T(8,128)S(1)} %get-tuple-element.19, f32[18,4,8,128]{3,2,1,0:T(8,128)} %param.5), kind=kLoop, calls=%fused_computation.27 | loop fusion | flops 159718 | bytes 229480 | tf_op jit(solution)/shard_map/reduce_min | solution.py:415
  4.2 0.7 convert_element_type.34
  4.9 0.8 log_subtract_fusion
  5.8 0.1 convert_reduce_fusion
  5.9 2.4 %fusion.weight_ref = bf16[4096,256]{1,0:T(8,128)(2,1)S(1)} fusion(s32[4096]{0:T(1024)} %bitcast.71, bf16[4096]{0:T(1024)(128)(2,1)S(1)} %fusion.26), kind=kLoop, calls=%fused_computation.3 | loop fusion | flops 2097152 | bytes 2121728 | tf_op jit(solution)/shard_map/jit(_where)/select_n | solution.py:419
  8.3 0.0 copy-start
  8.4 4.9 %copy-done = bf16[1681,4,8,128]{3,2,1,0:T(8,128)(2,1)S(1)} copy-done((bf16[1681,4,8,128]{3,2,1,0:T(8,128)(2,1)S(1)}, bf16[1681,4,8,128]{3,2,1,0:T(8,128)(2,1)}, u32[]{:S(2)}) %copy-start) | copy-done | bytes 13770776
  13.3 0.0 copy-start.1
  13.3 9.0 %shard_map.68 = (bf16[1681,4096]{1,0:T(8,128)(2,1)}, f32[1792,256]{1,0:T(8,128)S(1)}) custom-call(bf16[1681,32,128]{2,1,0:T(8,128)(2,1)S(1)} %bitcast.67, bf16[4096,256]{1,0:T(8,128)(2,1)S(1)} %fusion.weight_ref), custom_call_target="tpu_custom_call" | custom-call | tf_op jit(solution)/shard_map/pallas_call | solution.py:360
  22.3 0.0 copy-start.4
  22.3 0.1 select_maximum_fusion.1
  22.4 0.1 pad_maximum_fusion.4
  22.4 0.1 broadcast_add_fusion
  22.5 0.1 exponential_select_fusion
  22.7 0.0 copy-done.1
  22.7 53.9 %shard_map.69 = (bf16[8,4,64,256]{3,2,1,0:T(8,128)(2,1)S(1)}, f32[8,256]{1,0:T(8,128)S(1)}, bf16[2,160,128]{2,1,0:T(8,128)(2,1)S(1)}) custom-call(f32[8,4,56,256]{3,2,1,0:T(8,128)S(1)} %bitcast.68, f32[8,256]{1,0:T(8,128)S(1)} %select_maximum_fusion.small_ref, f32[56,1024]{1,0:T(8,128)S(1)} %get-tuple-element.33.grow_in_ref, ...), custom_call_target="tpu_custom_call" | custom-call | tf_op jit(solution)/shard_map/pallas_call | solution.py:313
  76.6 0.1 slice.130
  76.7 0.0 copy-done.4
  76.7 0.0 copy-start.2
  76.7 9.6 %fusion.1 = f32[4096]{0:T(1024)S(1)} fusion(bf16[1681,4096]{1,0:T(8,128)(2,1)} %get-tuple-element.10, s32[4096]{0:T(1024)S(1)} %bitcast.72, bf16[1792,256]{1,0:T(8,128)(2,1)S(1)} %bitcast.70), kind=kOutput, calls=%fused_computation.4 | convolution fusion | flops 3528454144 | bytes 14667776 | tf_op jit(solution)/shard_map/dot_general | solution.py:453
  86.4 0.0 copy-start.3
  86.4 8.9 %collective-permute-start.1 = (f32[1,8,128]{2,1,0:T(8,128)S(1)}, f32[1,8,128]{2,1,0:T(8,128)S(1)}, u32[]{:S(2)}, u32[]{:S(2)}) collective-permute-start(f32[1,8,128]{2,1,0:T(8,128)S(1)} %get-tuple-element.25), channel_id=1, source_target_pairs={{0,1},{1,2},{2,3},{3,4},{4,5},{5,6},{6,7},{7,8},{8,9},{9,10},{10,1... | collective-permute-start | bytes 12296 | tf_op jit(solution)/shard_map/ppermute | solution.py:29
  95.3 1.9 %collective-permute-start = (f32[1,8,128]{2,1,0:T(8,128)S(1)}, f32[1,8,128]{2,1,0:T(8,128)S(1)}, u32[]{:S(2)}, u32[]{:S(2)}) collective-permute-start(f32[1,8,128]{2,1,0:T(8,128)S(1)} %get-tuple-element.24), channel_id=1, source_target_pairs={{1,0},{2,1},{3,2},{4,3},{5,4},{6,5},{7,6},{8,7},{9,8},{10,9},{11,1... | collective-permute-start | bytes 12296 | tf_op jit(solution)/shard_map/ppermute | solution.py:31
  97.2 0.1 maximum_convert_fusion
  97.4 0.0 copy-done.2
  97.4 0.1 slice_bitcast_fusion.6
  97.5 0.0 collective-permute-done.1
  97.5 4.5 %collective-permute-done = f32[1,8,128]{2,1,0:T(8,128)S(1)} collective-permute-done((f32[1,8,128]{2,1,0:T(8,128)S(1)}, f32[1,8,128]{2,1,0:T(8,128)S(1)}, u32[]{:S(2)}, u32[]{:S(2)}) %collective-permute-start) | collective-permute-done | bytes 4128 | tf_op jit(solution)/shard_map/ppermute | solution.py:31
  102.0 0.1 fusion.9
  102.1 0.0 copy-done.3
  102.1 0.0 copy-start.5
  102.2 0.7 copy-done.5
  (18 shorter events, 0.2 us)
Async XLA Ops:
  8.3 4.9 %copy-start = (bf16[1681,4,8,128]{3,2,1,0:T(8,128)(2,1)S(1)}, bf16[1681,4,8,128]{3,2,1,0:T(8,128)(2,1)}, u32[]{:S(2)}) copy-start(bf16[1681,4,8,128]{3,2,1,0:T(8,128)(2,1)} %param.6) | copy-start | bytes 41312260
  13.3 9.4 %copy-start.1 = (f32[1024]{0:T(1024)S(1)}, f32[1024]{0:T(1024)}, u32[]{:S(2)}) copy-start(f32[1024]{0:T(1024)} %param.9) | copy-start | bytes 12292
  22.3 54.4 %copy-start.4 = (s32[4,8,128]{2,1,0:T(8,128)S(1)}, s32[4,8,128]{2,1,0:T(8,128)}, u32[]{:S(2)}) copy-start(s32[4,8,128]{2,1,0:T(8,128)} %param.7) | copy-start | bytes 49156
  76.7 20.7 %copy-start.2 = (f32[18,4,8,128]{3,2,1,0:T(8,128)S(1)}, f32[18,4,8,128]{3,2,1,0:T(8,128)}, u32[]{:S(2)}) copy-start(f32[18,4,8,128]{3,2,1,0:T(8,128)} %param.5) | copy-start | bytes 884740
  86.4 15.8 %copy-start.3 = (f32[4,8,128]{2,1,0:T(8,128)}, f32[4,8,128]{2,1,0:T(8,128)S(1)}, u32[]{:S(2)}) copy-start(f32[4,8,128]{2,1,0:T(8,128)S(1)} %get-tuple-element.27) | copy-start | bytes 49156
  86.4 11.1 %collective-permute-start.1 = (f32[1,8,128]{2,1,0:T(8,128)S(1)}, f32[1,8,128]{2,1,0:T(8,128)S(1)}, u32[]{:S(2)}, u32[]{:S(2)}) collective-permute-start(f32[1,8,128]{2,1,0:T(8,128)S(1)} %get-tuple-element.25), channel_id=1, source_target_pairs={{0,1},{1,2},{2,3},{3,4},{4,5},{5,6},{6,7},{7,8},{8,9},{9,10},{10,1... | collective-permute-start | bytes 12296 | tf_op jit(solution)/shard_map/ppermute | solution.py:29
  95.3 6.7 %collective-permute-start = (f32[1,8,128]{2,1,0:T(8,128)S(1)}, f32[1,8,128]{2,1,0:T(8,128)S(1)}, u32[]{:S(2)}, u32[]{:S(2)}) collective-permute-start(f32[1,8,128]{2,1,0:T(8,128)S(1)} %get-tuple-element.24), channel_id=1, source_target_pairs={{1,0},{2,1},{3,2},{4,3},{5,4},{6,5},{7,6},{8,7},{9,8},{10,9},{11,1... | collective-permute-start | bytes 12296 | tf_op jit(solution)/shard_map/ppermute | solution.py:31
  102.1 0.7 copy-start.5

commit v5 on v4

--- a/solution.py
+++ b/solution.py
@@ -341,7 +341,7 @@
     )(parts, small, grow_in, grow_out, radius, edges)
 
 
-TILE = 224
+TILE = 128
 
 
 def moment_kernel(harm_count, harm_ref, weight_ref, flat_ref, part_ref):

time: 104 us -> 106 us (1.019)
  Pallas kernels: 62.9 us -> 65.1 us
    pallas_call x1, Pallas kernels: 9 us -> 11.2 us  [flat_and_moments(): pl.pallas_call(functools.partial(moment_kernel, harm_count), grid=(steps,...]
where the time goes in v5:
time: 106 us; the launch traced here: 105 us
  Pallas kernels  65.1 us (61%)
  starting transfers between devices  10.8 us (10%)
  matrix products  9.64 us (9%)
  other arithmetic  7.71 us (7%)
  local copies, waits for them, and re-layouts  6.45 us (6%)
  waiting for transfers between devices  4.49 us (4%)
    pallas_call x1, Pallas kernels, exchange(): pl.pallas_call(functools.partial(exchange_kernel, outer), out_shape=(jax....  53.9 us
    pallas_call x1, Pallas kernels, flat_and_moments(): pl.pallas_call(functools.partial(moment_kernel, harm_count), grid=(steps,...  11.2 us
    dot_general x1, matrix products, per_device(): product = jnp.dot(shell_mine, flat_harm, preferred_element_type=jnp.float32)  9.64 us
    ppermute x1, starting transfers between devices, padded_2(): lax.ppermute(tail, axis, [(i, (i + 1) % count) for i in range(ends)])  8.89 us
    unnamed x13, local copies, waits for them, and re-layouts  5.64 us
    ppermute x1, waiting for transfers between devices, padded_2(): lax.ppermute(head, axis, [((i + 1) % count, i) for i in range(ends)])  4.48 us
    select_n x1, other arithmetic, per_device(): jnp.where(slot_flat[:, None] == jnp.arange(listed, dtype=jnp.int32)[None,...  2.44 us
  transfers between devices with their start and end apart: 2, of which 1 were waited for; matrix products, arithmetic and copies ran while one was open for 0% of the time, Pallas kernels for 0%

profile of v5, /device:TPU:15, one launch (start us, length us, event | category | flops | bytes accessed | tf_op | source)
XLA Modules:
  0.0 105.1 jit_solution(11792859623728809560)
XLA Ops:
  0.6 0.7 fusion.26
  1.4 0.7 divide_convert_fusion
  2.1 1.0 convert.6
  3.1 1.1 %fusion.14 = (f32[13]{0:T(128)S(1)}, f32[13]{0:T(128)S(1)}) fusion(f32[4,8,128]{2,1,0:T(8,128)S(1)} %get-tuple-element.19, f32[18,4,8,128]{3,2,1,0:T(8,128)} %param.5), kind=kLoop, calls=%fused_computation.27 | loop fusion | flops 159718 | bytes 229480 | tf_op jit(solution)/shard_map/reduce_min | solution.py:415
  4.2 0.7 convert_element_type.34
  4.9 0.8 log_subtract_fusion
  5.8 0.1 convert_reduce_fusion
  5.9 2.4 %fusion.weight_ref = bf16[4096,256]{1,0:T(8,128)(2,1)S(1)} fusion(s32[4096]{0:T(1024)} %bitcast.71, bf16[4096]{0:T(1024)(128)(2,1)S(1)} %fusion.26), kind=kLoop, calls=%fused_computation.3 | loop fusion | flops 2097152 | bytes 2121728 | tf_op jit(solution)/shard_map/jit(_where)/select_n | solution.py:419
  8.3 0.0 copy-start
  8.4 4.9 %copy-done = bf16[1681,4,8,128]{3,2,1,0:T(8,128)(2,1)S(1)} copy-done((bf16[1681,4,8,128]{3,2,1,0:T(8,128)(2,1)S(1)}, bf16[1681,4,8,128]{3,2,1,0:T(8,128)(2,1)}, u32[]{:S(2)}) %copy-start) | copy-done | bytes 13770776
  13.3 0.0 copy-start.1
  13.3 11.2 %shard_map.68 = (bf16[1681,4096]{1,0:T(8,128)(2,1)}, f32[1792,256]{1,0:T(8,128)S(1)}) custom-call(bf16[1681,32,128]{2,1,0:T(8,128)(2,1)S(1)} %bitcast.67, bf16[4096,256]{1,0:T(8,128)(2,1)S(1)} %fusion.weight_ref), custom_call_target="tpu_custom_call" | custom-call | tf_op jit(solution)/shard_map/pallas_call | solution.py:360
  24.5 0.0 copy-start.4
  24.5 0.1 select_maximum_fusion.1
  24.6 0.1 pad_maximum_fusion.4
  24.6 0.1 broadcast_add_fusion
  24.7 0.1 exponential_select_fusion
  24.9 0.0 copy-done.1
  24.9 53.9 %shard_map.69 = (bf16[8,4,64,256]{3,2,1,0:T(8,128)(2,1)S(1)}, f32[8,256]{1,0:T(8,128)S(1)}, bf16[2,160,128]{2,1,0:T(8,128)(2,1)S(1)}) custom-call(f32[8,4,56,256]{3,2,1,0:T(8,128)S(1)} %bitcast.68, f32[8,256]{1,0:T(8,128)S(1)} %select_maximum_fusion.small_ref, f32[56,1024]{1,0:T(8,128)S(1)} %get-tuple-element.33.grow_in_ref, ...), custom_call_target="tpu_custom_call" | custom-call | tf_op jit(solution)/shard_map/pallas_call | solution.py:313
  78.8 0.1 slice.130
  78.9 0.0 copy-done.4
  78.9 0.0 copy-start.2
  78.9 9.6 %fusion.1 = f32[4096]{0:T(1024)S(1)} fusion(bf16[1681,4096]{1,0:T(8,128)(2,1)} %get-tuple-element.10, s32[4096]{0:T(1024)S(1)} %bitcast.72, bf16[1792,256]{1,0:T(8,128)(2,1)S(1)} %bitcast.70), kind=kOutput, calls=%fused_computation.4 | convolution fusion | flops 3528454144 | bytes 14667776 | tf_op jit(solution)/shard_map/dot_general | solution.py:453
  88.6 0.0 copy-start.3
  88.6 8.9 %collective-permute-start.1 = (f32[1,8,128]{2,1,0:T(8,128)S(1)}, f32[1,8,128]{2,1,0:T(8,128)S(1)}, u32[]{:S(2)}, u32[]{:S(2)}) collective-permute-start(f32[1,8,128]{2,1,0:T(8,128)S(1)} %get-tuple-element.25), channel_id=1, source_target_pairs={{0,1},{1,2},{2,3},{3,4},{4,5},{5,6},{6,7},{7,8},{8,9},{9,10},{10,1... | collective-permute-start | bytes 12296 | tf_op jit(solution)/shard_map/ppermute | solution.py:29
  97.5 1.9 %collective-permute-start = (f32[1,8,128]{2,1,0:T(8,128)S(1)}, f32[1,8,128]{2,1,0:T(8,128)S(1)}, u32[]{:S(2)}, u32[]{:S(2)}) collective-permute-start(f32[1,8,128]{2,1,0:T(8,128)S(1)} %get-tuple-element.24), channel_id=1, source_target_pairs={{1,0},{2,1},{3,2},{4,3},{5,4},{6,5},{7,6},{8,7},{9,8},{10,9},{11,1... | collective-permute-start | bytes 12296 | tf_op jit(solution)/shard_map/ppermute | solution.py:31
  99.4 0.1 maximum_convert_fusion
  99.6 0.0 copy-done.2
  99.6 0.1 slice_bitcast_fusion.6
  99.7 0.0 collective-permute-done.1
  99.7 4.5 %collective-permute-done = f32[1,8,128]{2,1,0:T(8,128)S(1)} collective-permute-done((f32[1,8,128]{2,1,0:T(8,128)S(1)}, f32[1,8,128]{2,1,0:T(8,128)S(1)}, u32[]{:S(2)}, u32[]{:S(2)}) %collective-permute-start) | collective-permute-done | bytes 4128 | tf_op jit(solution)/shard_map/ppermute | solution.py:31
  104.2 0.1 fusion.9
  104.4 0.0 copy-done.3
  104.4 0.0 copy-start.5
  104.4 0.7 copy-done.5
  (18 shorter events, 0.2 us)
Async XLA Ops:
  8.3 4.9 %copy-start = (bf16[1681,4,8,128]{3,2,1,0:T(8,128)(2,1)S(1)}, bf16[1681,4,8,128]{3,2,1,0:T(8,128)(2,1)}, u32[]{:S(2)}) copy-start(bf16[1681,4,8,128]{3,2,1,0:T(8,128)(2,1)} %param.6) | copy-start | bytes 41312260
  13.3 11.6 %copy-start.1 = (f32[1024]{0:T(1024)S(1)}, f32[1024]{0:T(1024)}, u32[]{:S(2)}) copy-start(f32[1024]{0:T(1024)} %param.9) | copy-start | bytes 12292
  24.5 54.4 %copy-start.4 = (s32[4,8,128]{2,1,0:T(8,128)S(1)}, s32[4,8,128]{2,1,0:T(8,128)}, u32[]{:S(2)}) copy-start(s32[4,8,128]{2,1,0:T(8,128)} %param.7) | copy-start | bytes 49156
  78.9 20.7 %copy-start.2 = (f32[18,4,8,128]{3,2,1,0:T(8,128)S(1)}, f32[18,4,8,128]{3,2,1,0:T(8,128)}, u32[]{:S(2)}) copy-start(f32[18,4,8,128]{3,2,1,0:T(8,128)} %param.5) | copy-start | bytes 884740
  88.6 15.8 %copy-start.3 = (f32[4,8,128]{2,1,0:T(8,128)}, f32[4,8,128]{2,1,0:T(8,128)S(1)}, u32[]{:S(2)}) copy-start(f32[4,8,128]{2,1,0:T(8,128)S(1)} %get-tuple-element.27) | copy-start | bytes 49156
  88.6 11.1 %collective-permute-start.1 = (f32[1,8,128]{2,1,0:T(8,128)S(1)}, f32[1,8,128]{2,1,0:T(8,128)S(1)}, u32[]{:S(2)}, u32[]{:S(2)}) collective-permute-start(f32[1,8,128]{2,1,0:T(8,128)S(1)} %get-tuple-element.25), channel_id=1, source_target_pairs={{0,1},{1,2},{2,3},{3,4},{4,5},{5,6},{6,7},{7,8},{8,9},{9,10},{10,1... | collective-permute-start | bytes 12296 | tf_op jit(solution)/shard_map/ppermute | solution.py:29
  97.5 6.7 %collective-permute-start = (f32[1,8,128]{2,1,0:T(8,128)S(1)}, f32[1,8,128]{2,1,0:T(8,128)S(1)}, u32[]{:S(2)}, u32[]{:S(2)}) collective-permute-start(f32[1,8,128]{2,1,0:T(8,128)S(1)} %get-tuple-element.24), channel_id=1, source_target_pairs={{1,0},{2,1},{3,2},{4,3},{5,4},{6,5},{7,6},{8,7},{9,8},{10,9},{11,1... | collective-permute-start | bytes 12296 | tf_op jit(solution)/shard_map/ppermute | solution.py:31
  104.4 0.7 copy-start.5
